TPU v7x, 128 devices: a whole 4x4x4 slice. The times are simulated.
128 devices in a mesh: dp: 32 (over x, z, core), ctx: 4 (over y).
Axes of the slice: x: 4, y: 4, z: 4, core: 2. Of those that a mesh axis runs over, the one named last changes fastest.
Arguments:
- activations: bfloat16 [32, 512, 1152], P('dp', 'ctx'), may hold values from -6 to 6
- cotangent: bfloat16 [32, 512, 1152], P('dp', 'ctx'), may hold values from -6 to 6
- segments: int32 [32, 512], P('dp'), may hold values from 0 to 4, as said below
- in_gain: bfloat16 [1152], P(('dp', 'ctx')), may hold values from -0.5 to 0.5
- query_gain: bfloat16 [256], P(('dp', 'ctx')), may hold values from -0.5 to 0.5
- key_gain: bfloat16 [256], P(('dp', 'ctx')), may hold values from -0.5 to 0.5
- post_attn_gain: bfloat16 [1152], P(('dp', 'ctx')), may hold values from -0.5 to 0.5
- pre_ff_gain: bfloat16 [1152], P(('dp', 'ctx')), may hold values from -0.5 to 0.5
- post_ff_gain: bfloat16 [1152], P(('dp', 'ctx')), may hold values from -0.5 to 0.5
- w_query: bfloat16 [1152, 1024], P(('dp', 'ctx')), may hold values from -0.1875 to 0.1875
- w_key: bfloat16 [1152, 256], P(('dp', 'ctx')), may hold values from -0.1875 to 0.1875
- w_value: bfloat16 [1152, 256], P(('dp', 'ctx')), may hold values from -0.1875 to 0.1875
- w_out: bfloat16 [1024, 1152], P(('dp', 'ctx')), may hold values from -0.1875 to 0.1875
- w_gate: bfloat16 [1152, 6912], P(('dp', 'ctx')), may hold values from -0.1875 to 0.1875
- w_up: bfloat16 [1152, 6912], P(('dp', 'ctx')), may hold values from -0.1875 to 0.1875
- w_down: bfloat16 [6912, 1152], P(('dp', 'ctx')), may hold values from -0.078125 to 0.078125
Outputs:
- output: bfloat16 [32, 512, 1152], P('dp', 'ctx')
- input_grad: float32 [32, 512, 1152], P('dp', 'ctx')
- in_gain_grad: float32 [1152], P(('dp', 'ctx'))
- query_gain_grad: float32 [256], P(('dp', 'ctx'))
- key_gain_grad: float32 [256], P(('dp', 'ctx'))
- post_attn_gain_grad: float32 [1152], P(('dp', 'ctx'))
- pre_ff_gain_grad: float32 [1152], P(('dp', 'ctx'))
- post_ff_gain_grad: float32 [1152], P(('dp', 'ctx'))
- w_query_grad: float32 [1152, 1024], P(('dp', 'ctx'))
- w_key_grad: float32 [1152, 256], P(('dp', 'ctx'))
- w_value_grad: float32 [1152, 256], P(('dp', 'ctx'))
- w_out_grad: float32 [1024, 1152], P(('dp', 'ctx'))
- w_gate_grad: float32 [1152, 6912], P(('dp', 'ctx'))
- w_up_grad: float32 [1152, 6912], P(('dp', 'ctx'))
- w_down_grad: float32 [6912, 1152], P(('dp', 'ctx'))
Inputs may be any that keep to these rules, and one draw needn't show every extreme that they name: `segments`: segment numbers never fall along a sequence and may skip values; in every sequence one document begins within the first 64 tokens and ends within the last 64 tokens.
All inputs are finite; a program needn't handle non-finite values.
Results may differ from a plain program's by a relative error of at most 0.035.
Values may be sent and summed in bfloat16 or wider, within the bound.
No kernel may reach another device: no remote copies, remote signals or barrier semaphores. Data moves between devices by JAX's collectives and lax.ppermute only.
A program may use at most 256 MiB of HBM per device.

v0:
```python
import math

import jax
import jax.numpy as jnp
from jax import lax
from jax.sharding import PartitionSpec as P

norm_eps = 1e-06
rope_base = 1000000.0
score_scale = 0.0625
far_below = -1e30


def rms_norm(values, gain):
    factor = lax.rsqrt(jnp.mean(values * values, axis=-1, keepdims=True) + norm_eps)
    return values * factor * (1.0 + gain)


def rotate(values, cosine, sine):
    half_dim = values.shape[-1] // 2
    first_half = values[..., :half_dim]
    second_half = values[..., half_dim:]
    return jnp.concatenate(
        [first_half * cosine - second_half * sine, second_half * cosine + first_half * sine],
        axis=-1,
    )


def rope_tables(positions, head_dim):
    freq_index = jnp.arange(head_dim // 2, dtype=jnp.float32)
    inverse = jnp.exp(freq_index * (-2.0 / head_dim) * math.log(rope_base))
    angles = positions.astype(jnp.float32)[:, None] * inverse[None, :]
    return (jnp.cos(angles), jnp.sin(angles))


def gated_unit(gate_pre, up_pre):
    return jax.nn.gelu(gate_pre, approximate=True) * up_pre


def contract_rows(left, right):
    return lax.dot_general(
        left, right, (((0,), (0,)), ((), ())), preferred_element_type=jnp.float32
    )


def contract_cols(left, right):
    return lax.dot_general(
        left, right, (((1,), (1,)), ((), ())), preferred_element_type=jnp.float32
    )


def split_owners(term, outer, inner):
    return term.reshape((outer, inner, term.shape[0] // (outer * inner)) + term.shape[1:])


def join_owners(term):
    return term.reshape((term.shape[2],) + term.shape[3:])


def block_scores(query_blk, segment_blk, place_blk, key_all, segment_all):
    key_places = jnp.arange(key_all.shape[0], dtype=jnp.int32)
    scores = (
        jnp.einsum("thd,kd->htk", query_blk, key_all, preferred_element_type=jnp.float32)
        * score_scale
    )
    allowed = (segment_blk[:, None] == segment_all[None, :]) & (
        place_blk[:, None] >= key_places[None, :]
    )
    return (jnp.where(allowed[None], scores, far_below), allowed)


def attend_block(query_blk, segment_blk, place_blk, key_all, value_all, segment_all):
    scores, allowed = block_scores(query_blk, segment_blk, place_blk, key_all, segment_all)
    top_score = jnp.max(scores, axis=-1, keepdims=True)
    weight = jnp.exp(scores - top_score)
    total = jnp.sum(weight, axis=-1, keepdims=True)
    prob_low = (weight / total).astype(jnp.bfloat16)
    attended = jnp.einsum("htk,kd->thd", prob_low, value_all, preferred_element_type=jnp.float32)
    return (attended, top_score[..., 0] + jnp.log(total[..., 0]))


def attend_back(
    query_blk, grad_blk, segment_blk, place_blk, log_total, key_all, value_all, segment_all
):
    scores, allowed = block_scores(query_blk, segment_blk, place_blk, key_all, segment_all)
    prob = jnp.where(allowed[None], jnp.exp(scores - log_total[..., None]), 0.0)
    prob_low = prob.astype(jnp.bfloat16)
    grad_prob = jnp.einsum("thd,kd->htk", grad_blk, value_all, preferred_element_type=jnp.float32)
    shift_term = jnp.sum(prob * grad_prob, axis=-1, keepdims=True)
    grad_scores = (prob * (grad_prob - shift_term)).astype(jnp.bfloat16)
    grad_query = (
        jnp.einsum("htk,kd->thd", grad_scores, key_all, preferred_element_type=jnp.float32)
        * score_scale
    )
    grad_key = (
        jnp.einsum("htk,thd->kd", grad_scores, query_blk, preferred_element_type=jnp.float32)
        * score_scale
    )
    grad_value = jnp.einsum("htk,thd->kd", prob_low, grad_blk, preferred_element_type=jnp.float32)
    return (grad_query, grad_key, grad_value)


def local(
    activations,
    cotangent,
    segments,
    in_gain,
    query_gain,
    key_gain,
    post_attn_gain,
    pre_ff_gain,
    post_ff_gain,
    w_query,
    w_key,
    w_value,
    w_out,
    w_gate,
    w_up,
    w_down,
):
    attn_full = (
        lax.all_gather(in_gain, ("dp", "ctx"), axis=0, tiled=True),
        lax.all_gather(query_gain, ("dp", "ctx"), axis=0, tiled=True),
        lax.all_gather(key_gain, ("dp", "ctx"), axis=0, tiled=True),
        lax.all_gather(post_attn_gain, ("dp", "ctx"), axis=0, tiled=True),
        lax.all_gather(w_query, ("dp", "ctx"), axis=0, tiled=True),
        lax.all_gather(w_key, ("dp", "ctx"), axis=0, tiled=True),
        lax.all_gather(w_value, ("dp", "ctx"), axis=0, tiled=True),
        lax.all_gather(w_out, ("dp", "ctx"), axis=0, tiled=True),
    )
    (
        full_in_gain,
        full_query_gain,
        full_key_gain,
        full_post_attn,
        full_query,
        full_key,
        full_value,
        full_out,
    ) = attn_full
    inputs = activations[0].astype(jnp.float32)
    segment_all = segments[0]
    tok_count = inputs.shape[0]
    head_dim = full_key_gain.shape[0]
    heads = full_query.shape[1] // head_dim
    first_place = lax.axis_index("ctx") * tok_count
    place_rows = first_place + jnp.arange(tok_count, dtype=jnp.int32)
    segment_rows = lax.dynamic_slice_in_dim(segment_all, first_place, tok_count)
    earlier = jnp.sum((segment_all[None, :] < segment_rows[:, None]).astype(jnp.int32), axis=1)
    cosine, sine = rope_tables(place_rows - earlier, head_dim)
    gain_in = full_in_gain.astype(jnp.float32)
    gain_query = full_query_gain.astype(jnp.float32)
    gain_key = full_key_gain.astype(jnp.float32)
    gain_post_attn = full_post_attn.astype(jnp.float32)
    normed, in_pull = jax.vjp(rms_norm, inputs, gain_in)
    normed_low = normed.astype(jnp.bfloat16)
    query_raw = jnp.dot(normed_low, full_query, preferred_element_type=jnp.float32).reshape(
        tok_count, heads, head_dim
    )
    key_raw = jnp.dot(normed_low, full_key, preferred_element_type=jnp.float32)
    value_low = jnp.dot(normed_low, full_value, preferred_element_type=jnp.float32).astype(
        jnp.bfloat16
    )

    def prepare(query_in, key_in, query_scale, key_scale):
        rotated_query = rotate(
            rms_norm(query_in, query_scale), cosine[:, None, :], sine[:, None, :]
        )
        rotated_key = rotate(rms_norm(key_in, key_scale), cosine, sine)
        return (rotated_query, rotated_key)

    (queries, key_rows), prepare_pull = jax.vjp(prepare, query_raw, key_raw, gain_query, gain_key)
    query_low = queries.astype(jnp.bfloat16)
    key_low = key_rows.astype(jnp.bfloat16)
    key_all, value_all = (
        lax.all_gather(key_low, "ctx", axis=0, tiled=True),
        lax.all_gather(value_low, "ctx", axis=0, tiled=True),
    )
    length = key_all.shape[0]
    block = math.gcd(tok_count, max(1, 512 // heads))
    count = tok_count // block
    query_blocks = query_low.reshape(count, block, heads, head_dim)
    segment_blocks = segment_rows.reshape(count, block)
    place_blocks = place_rows.reshape(count, block)

    def forward_block(item):
        return attend_block(item[0], item[1], item[2], key_all, value_all, segment_all)

    attended, log_total = lax.map(forward_block, (query_blocks, segment_blocks, place_blocks))
    attended_low = attended.reshape(tok_count, heads * head_dim).astype(jnp.bfloat16)
    attn_out = jnp.dot(attended_low, full_out, preferred_element_type=jnp.float32)
    post_attn, post_attn_pull = jax.vjp(rms_norm, attn_out, gain_post_attn)
    middle = inputs + post_attn
    ffn_full = (
        lax.all_gather(pre_ff_gain, ("dp", "ctx"), axis=0, tiled=True),
        lax.all_gather(post_ff_gain, ("dp", "ctx"), axis=0, tiled=True),
        lax.all_gather(w_gate, ("dp", "ctx"), axis=0, tiled=True),
        lax.all_gather(w_up, ("dp", "ctx"), axis=0, tiled=True),
        lax.all_gather(w_down, ("dp", "ctx"), axis=0, tiled=True),
    )
    full_pre, full_post, full_gate, full_up, full_down = ffn_full
    normed_ff, pre_pull = jax.vjp(rms_norm, middle, full_pre.astype(jnp.float32))
    normed_ff_low = normed_ff.astype(jnp.bfloat16)
    gate_pre = jnp.dot(normed_ff_low, full_gate, preferred_element_type=jnp.float32)
    up_pre = jnp.dot(normed_ff_low, full_up, preferred_element_type=jnp.float32)
    mixed, gated_pull = jax.vjp(gated_unit, gate_pre, up_pre)
    mixed_low = mixed.astype(jnp.bfloat16)
    branch_out = jnp.dot(mixed_low, full_down, preferred_element_type=jnp.float32)
    post_ff, post_pull = jax.vjp(rms_norm, branch_out, full_post.astype(jnp.float32))
    output = (middle + post_ff).astype(jnp.bfloat16)
    back_ffn = (
        lax.all_gather(w_gate, ("dp", "ctx"), axis=0, tiled=True),
        lax.all_gather(w_up, ("dp", "ctx"), axis=0, tiled=True),
        lax.all_gather(w_down, ("dp", "ctx"), axis=0, tiled=True),
    )
    back_attn = (
        lax.all_gather(w_query, ("dp", "ctx"), axis=0, tiled=True),
        lax.all_gather(w_key, ("dp", "ctx"), axis=0, tiled=True),
        lax.all_gather(w_value, ("dp", "ctx"), axis=0, tiled=True),
        lax.all_gather(w_out, ("dp", "ctx"), axis=0, tiled=True),
    )
    back_gate, back_up, back_down = back_ffn
    back_query, back_key, back_value, back_out = back_attn
    grad_output = cotangent[0].astype(jnp.float32)
    grad_branch, grad_post_ff = post_pull(grad_output)
    grad_branch_low = grad_branch.astype(jnp.bfloat16)
    grad_mixed = contract_cols(grad_branch_low, back_down)
    down_term = contract_rows(mixed_low, grad_branch_low)
    grad_gate, grad_up = gated_pull(grad_mixed)
    grad_gate_low = grad_gate.astype(jnp.bfloat16)
    grad_up_low = grad_up.astype(jnp.bfloat16)
    grad_normed_ff = contract_cols(grad_gate_low, back_gate) + contract_cols(grad_up_low, back_up)
    gate_term = contract_rows(normed_ff_low, grad_gate_low)
    up_term = contract_rows(normed_ff_low, grad_up_low)
    grad_middle_add, grad_pre_ff = pre_pull(grad_normed_ff)
    grad_middle = grad_output + grad_middle_add
    outer = lax.axis_size("dp")
    inner = lax.axis_size("ctx")
    owned = tuple(
        (
            split_owners(term, outer, inner)
            for term in (grad_pre_ff, grad_post_ff, gate_term, up_term, down_term)
        )
    )
    within = (
        lax.psum_scatter(
            owned[0].astype(jnp.bfloat16), "ctx", scatter_dimension=1, tiled=True
        ).astype(jnp.float32),
        lax.psum_scatter(
            owned[1].astype(jnp.bfloat16), "ctx", scatter_dimension=1, tiled=True
        ).astype(jnp.float32),
        lax.psum_scatter(
            owned[2].astype(jnp.bfloat16), "ctx", scatter_dimension=1, tiled=True
        ).astype(jnp.float32),
        lax.psum_scatter(
            owned[3].astype(jnp.bfloat16), "ctx", scatter_dimension=1, tiled=True
        ).astype(jnp.float32),
        lax.psum_scatter(
            owned[4].astype(jnp.bfloat16), "ctx", scatter_dimension=1, tiled=True
        ).astype(jnp.float32),
    )
    across = (
        lax.psum_scatter(
            within[0].astype(jnp.bfloat16), "dp", scatter_dimension=0, tiled=True
        ).astype(jnp.float32),
        lax.psum_scatter(
            within[1].astype(jnp.bfloat16), "dp", scatter_dimension=0, tiled=True
        ).astype(jnp.float32),
        lax.psum_scatter(
            within[2].astype(jnp.bfloat16), "dp", scatter_dimension=0, tiled=True
        ).astype(jnp.float32),
        lax.psum_scatter(
            within[3].astype(jnp.bfloat16), "dp", scatter_dimension=0, tiled=True
        ).astype(jnp.float32),
        lax.psum_scatter(
            within[4].astype(jnp.bfloat16), "dp", scatter_dimension=0, tiled=True
        ).astype(jnp.float32),
    )
    ffn_grads = tuple((join_owners(term) for term in across))
    grad_attn, grad_post_attn = post_attn_pull(grad_middle)
    grad_attn_low = grad_attn.astype(jnp.bfloat16)
    out_term = contract_rows(attended_low, grad_attn_low)
    grad_attended = contract_cols(grad_attn_low, back_out).astype(jnp.bfloat16)
    grad_attended = grad_attended.reshape(count, block, heads, head_dim)

    def backward_block(carry, item):
        grad_query, grad_key, grad_value = attend_back(
            item[0], item[1], item[2], item[3], item[4], key_all, value_all, segment_all
        )
        return ((carry[0] + grad_key, carry[1] + grad_value), grad_query)

    zero_rows = jnp.zeros((length, head_dim), jnp.float32)
    (key_sum_term, value_sum_term), grad_queries = lax.scan(
        backward_block,
        (zero_rows, zero_rows),
        (query_blocks, grad_attended, segment_blocks, place_blocks, log_total),
    )
    grad_key_rows, grad_value_rows = (
        lax.psum_scatter(
            key_sum_term.astype(jnp.bfloat16), "ctx", scatter_dimension=0, tiled=True
        ).astype(jnp.float32),
        lax.psum_scatter(
            value_sum_term.astype(jnp.bfloat16), "ctx", scatter_dimension=0, tiled=True
        ).astype(jnp.float32),
    )
    grad_value_low = grad_value_rows.astype(jnp.bfloat16)
    grad_query_raw, grad_key_raw, grad_query_gain, grad_key_gain = prepare_pull(
        (grad_queries.reshape(tok_count, heads, head_dim), grad_key_rows)
    )
    grad_query_low = grad_query_raw.reshape(tok_count, heads * head_dim).astype(jnp.bfloat16)
    grad_key_low = grad_key_raw.astype(jnp.bfloat16)
    query_weight_term = contract_rows(normed_low, grad_query_low)
    key_weight_term = contract_rows(normed_low, grad_key_low)
    value_weight_term = contract_rows(normed_low, grad_value_low)
    grad_normed = contract_cols(grad_query_low, back_query) + contract_cols(grad_key_low, back_key)
    grad_normed = grad_normed + contract_cols(grad_value_low, back_value)
    grad_input_add, grad_in_gain = in_pull(grad_normed)
    input_grad = grad_middle + grad_input_add
    attn_grads = (
        lax.psum_scatter(grad_in_gain, ("dp", "ctx"), scatter_dimension=0, tiled=True),
        lax.psum_scatter(grad_query_gain, ("dp", "ctx"), scatter_dimension=0, tiled=True),
        lax.psum_scatter(grad_key_gain, ("dp", "ctx"), scatter_dimension=0, tiled=True),
        lax.psum_scatter(grad_post_attn, ("dp", "ctx"), scatter_dimension=0, tiled=True),
        lax.psum_scatter(query_weight_term, ("dp", "ctx"), scatter_dimension=0, tiled=True),
        lax.psum_scatter(key_weight_term, ("dp", "ctx"), scatter_dimension=0, tiled=True),
        lax.psum_scatter(value_weight_term, ("dp", "ctx"), scatter_dimension=0, tiled=True),
        lax.psum_scatter(out_term, ("dp", "ctx"), scatter_dimension=0, tiled=True),
    )
    return (
        output[None],
        input_grad[None],
        attn_grads[0],
        attn_grads[1],
        attn_grads[2],
        attn_grads[3],
        ffn_grads[0],
        ffn_grads[1],
        attn_grads[4],
        attn_grads[5],
        attn_grads[6],
        attn_grads[7],
        ffn_grads[2],
        ffn_grads[3],
        ffn_grads[4],
    )


def solution(mesh):
    placed = (
        P("dp", "ctx", None),
        P("dp", "ctx", None),
        P("dp", None),
        P(("dp", "ctx")),
        P(("dp", "ctx")),
        P(("dp", "ctx")),
        P(("dp", "ctx")),
        P(("dp", "ctx")),
        P(("dp", "ctx")),
        P(("dp", "ctx"), None),
        P(("dp", "ctx"), None),
        P(("dp", "ctx"), None),
        P(("dp", "ctx"), None),
        P(("dp", "ctx"), None),
        P(("dp", "ctx"), None),
        P(("dp", "ctx"), None),
    )
    return jax.shard_map(
        local,
        mesh=mesh,
        in_specs=placed,
        out_specs=(
            P("dp", "ctx", None),
            P("dp", "ctx", None),
            P(("dp", "ctx")),
            P(("dp", "ctx")),
            P(("dp", "ctx")),
            P(("dp", "ctx")),
            P(("dp", "ctx")),
            P(("dp", "ctx")),
            P(("dp", "ctx"), None),
            P(("dp", "ctx"), None),
            P(("dp", "ctx"), None),
            P(("dp", "ctx"), None),
            P(("dp", "ctx"), None),
            P(("dp", "ctx"), None),
            P(("dp", "ctx"), None),
        ),
        check_vma=False,
    )
```

profile of v0, /device:TPU:1, one launch (start us, length us, event | category | flops | bytes accessed | tf_op | source)
XLA Modules:
  0.0 1473.5 jit_solution(15732607476527228129)
XLA Ops:
  10.7 65.3 %all-gather.1 = bf16[128,9,256]{2,1,0:T(8,128)(2,1)S(1)} all-gather(bf16[1,9,256]{2,1,0:T(8,128)(2,1)} %bitcast.183), channel_id=1, replica_groups=mesh['dp'=32,'ctx'=4] {'dp','ctx'}, dimensions={0}, use_global_device_ids=true | all-gather | bytes 594432 | tf_op jit(solution)/shard_map/all_gather | solution.py:127
  76.2 61.9 %all-gather = bf16[128,9,256]{2,1,0:T(8,128)(2,1)S(1)} all-gather(bf16[1,9,256]{2,1,0:T(8,128)(2,1)} %bitcast.184), channel_id=1, replica_groups=mesh['dp'=32,'ctx'=4] {'dp','ctx'}, dimensions={0}, use_global_device_ids=true | all-gather | bytes 594432 | tf_op jit(solution)/shard_map/all_gather | solution.py:128
  140.0 65.4 %all-reduce.23 = (bf16[1152]{0:T(1024)(128)(2,1)S(1)}, bf16[256]{0:T(256)(128)(2,1)S(1)}, bf16[256]{0:T(256)(128)(2,1)S(1)}, bf16[1152]{0:T(1024)(128)(2,1)S(1)}...) all-reduce(bf16[1152]{0:T(1024)(128)(2,1)S(1)} %dynamic-update-slic, ...), channel_id=1, replica_groups=mesh['dp'=32,'ctx'=4] {'dp','ctx'}, use_global_device_ids=true, to_apply=%add.4 | all-reduce | flops 5120 | bytes 20480
  219.5 12.4 all_gather.54
  249.8 22.4 %reshape.405 = bf16[1152,6912]{1,0:T(8,128)(2,1)} reshape(bf16[128,9,6912]{2,1,0:T(8,128)(2,1)} %all-gather.16.cloned.1.call-done) | data formatting | bytes 31850496
  272.2 78.1 %all-gather.18.cloned.1.call-done = bf16[128,9,6912]{2,1,0:T(8,128)(2,1)} async-done(((bf16[1,9,6912]{2,1,0:T(8,128)(2,1)}), bf16[128,9,6912]{2,1,0:T(8,128)(2,1)}) %all-gather.18.cloned.1.call-update) | async-done | bytes 15925264 | tf_op jit(solution)/shard_map/all_gather | solution.py:198
  350.3 22.4 %reshape.407 = bf16[1152,6912]{1,0:T(8,128)(2,1)} reshape(bf16[128,9,6912]{2,1,0:T(8,128)(2,1)} %all-gather.18.cloned.1.call-done) | data formatting | bytes 31850496
  388.9 43.2 %all-gather.20.cloned.1.call-done = bf16[128,54,1152]{2,1,0:T(8,128)(2,1)} async-done(((bf16[1,54,1152]{2,1,0:T(8,128)(2,1)}), bf16[128,54,1152]{2,1,0:T(8,128)(2,1)}) %all-gather.20.cloned.1.call-update) | async-done | bytes 15925264 | tf_op jit(solution)/shard_map/all_gather | solution.py:199
  432.1 18.5 %reshape.409 = bf16[6912,1152]{1,0:T(8,128)(2,1)} reshape(bf16[128,54,1152]{2,1,0:T(8,128)(2,1)} %all-gather.20.cloned.1.call-done) | data formatting | bytes 31850496
  511.6 21.0 %convert_element_type.213 = bf16[32,4,9,6912]{3,2,1,0:T(8,128)(2,1)} reshape(bf16[1152,6912]{1,0:T(8,128)(2,1)} %convolution_convert_fusion.1) | data formatting | bytes 31850496 | tf_op jit(solution)/shard_map/convert_element_type | solution.py:256
  532.6 19.4 %copy.80 = bf16[32,4,9,6912]{3,0,2,1:T(8,128)(2,1)} copy(bf16[32,4,9,6912]{3,2,1,0:T(8,128)(2,1)} %convert_element_type.213) | data formatting | bytes 31850496 | tf_op jit(solution)/shard_map/convert_element_type | solution.py:256
  561.3 20.6 %convert_element_type.211 = bf16[32,4,9,6912]{3,2,1,0:T(8,128)(2,1)} reshape(bf16[1152,6912]{1,0:T(8,128)(2,1)} %convolution_convert_fusion.2) | data formatting | bytes 31850496 | tf_op jit(solution)/shard_map/convert_element_type | solution.py:253
  581.9 19.8 %copy.78 = bf16[32,4,9,6912]{3,0,2,1:T(8,128)(2,1)} copy(bf16[32,4,9,6912]{3,2,1,0:T(8,128)(2,1)} %convert_element_type.211) | data formatting | bytes 31850496 | tf_op jit(solution)/shard_map/convert_element_type | solution.py:253
  610.5 18.5 %convert_element_type.215 = bf16[32,4,54,1152]{3,2,1,0:T(8,128)(2,1)} reshape(bf16[6912,1152]{1,0:T(8,128)(2,1)} %convolution_convert_fusion) | data formatting | bytes 31850496 | tf_op jit(solution)/shard_map/convert_element_type | solution.py:259
  629.0 15.4 %copy.82 = bf16[32,4,54,1152]{3,0,2,1:T(8,128)(2,1)} copy(bf16[32,4,54,1152]{3,2,1,0:T(8,128)(2,1)} %convert_element_type.215) | data formatting | bytes 31850496 | tf_op jit(solution)/shard_map/convert_element_type | solution.py:259
  659.7 33.0 %reduce-scatter.25.cloned.1.call-done = bf16[32,1,9,6912]{3,0,2,1:T(8,128)(2,1)} async-done(((bf16[32,4,9,6912]{3,0,2,1:T(8,128)(2,1)}), bf16[32,1,9,6912]{3,0,2,1:T(8,128)(2,1)}) %reduce-scatter.25.cloned.1.call-update) | async-done | bytes 3981328 | tf_op jit(solution)/shard_map/reduce_scatter | solution.py:255
  700.1 136.4 %reduce-scatter.21.cloned.1.call-done = bf16[32,1,9,6912]{3,0,2,1:T(8,128)(2,1)} async-done(((bf16[32,4,9,6912]{3,0,2,1:T(8,128)(2,1)}), bf16[32,1,9,6912]{3,0,2,1:T(8,128)(2,1)}) %reduce-scatter.21.cloned.1.call-update) | async-done | bytes 3981328 | tf_op jit(solution)/shard_map/reduce_scatter | solution.py:252
  843.9 136.1 %reduce-scatter.29.cloned.1.call-done = bf16[32,1,54,1152]{3,0,2,1:T(8,128)(2,1)} async-done(((bf16[32,4,54,1152]{3,0,2,1:T(8,128)(2,1)}), bf16[32,1,54,1152]{3,0,2,1:T(8,128)(2,1)}) %reduce-scatter.29.cloned.1.call-update) | async-done | bytes 3981328 | tf_op jit(solution)/shard_map/reduce_scatter | solution.py:258
  1001.5 22.0 %reduce-scatter.19.cloned.1.call-done = bf16[32,1,9]{0,2,1:T(8,128)(2,1)} async-done(((bf16[32,4,9]{0,2,1:T(8,128)(2,1)}), bf16[32,1,9]{0,2,1:T(8,128)(2,1)}) %reduce-scatter.19.cloned.1.call-update) | async-done | bytes 592 | tf_op jit(solution)/shard_map/reduce_scatter | solution.py:249
  1024.2 124.1 %all-reduce.24 = (bf16[32,1,9]{2,1,0:T(2,128)(2,1)S(1)}, bf16[32,1,9]{2,1,0:T(2,128)(2,1)S(1)}) all-reduce(bf16[32,1,9]{2,1,0:T(2,128)(2,1)S(1)} %copy.75, bf16[32,1,9]{2,1,0:T(2,128)(2,1)S(1)} %copy.77), channel_id=9, replica_groups=mesh['dp'=32,'ctx'=4] {'dp'}, use_global_device_ids=true, to_apply=%region_28.29.clone | all-reduce | flops 576 | bytes 2304
  1152.7 67.8 %all-reduce.21 = (f32[1152]{0:T(1024)S(1)}, f32[256]{0:T(256)S(1)}, f32[256]{0:T(256)S(1)}, f32[1152]{0:T(1024)S(1)}) all-reduce(f32[1152]{0:T(1024)S(1)} %get-tuple-element.86, f32[256]{0:T(256)S(1)} %get-tuple-element.70, f32[256]{0:T(256)S(1)} %get-tuple-element.88, ...), channel_id=4, replica_groups=mesh['dp'=32,'ctx'=4] {'dp','ctx'}, use_global_device_ids=true, to_apply=%region_19.20.clone | all-reduce | flops 2816 | bytes 22528
  1228.2 60.6 %reduce-scatter.27.cloned.1.call-done = bf16[1,1,9,6912]{3,2,1,0:T(8,128)(2,1)} async-done(((bf16[32,1,9,6912]{3,2,1,0:T(8,128)(2,1)}), bf16[1,1,9,6912]{3,2,1,0:T(8,128)(2,1)}) %reduce-scatter.27.cloned.1.call-update) | async-done | bytes 124432 | tf_op jit(solution)/shard_map/reduce_scatter | solution.py:272
  1290.5 89.6 %reduce-scatter.23.cloned.1.call-done = bf16[1,1,9,6912]{3,2,1,0:T(8,128)(2,1)} async-done(((bf16[32,1,9,6912]{3,2,1,0:T(8,128)(2,1)}), bf16[1,1,9,6912]{3,2,1,0:T(8,128)(2,1)}) %reduce-scatter.23.cloned.1.call-update) | async-done | bytes 124432 | tf_op jit(solution)/shard_map/reduce_scatter | solution.py:269
  1381.9 83.3 %reduce-scatter.31.cloned.1.call-done = bf16[1,1,54,1152]{3,2,1,0:T(8,128)(2,1)} async-done(((bf16[32,1,54,1152]{3,2,1,0:T(8,128)(2,1)}), bf16[1,1,54,1152]{3,2,1,0:T(8,128)(2,1)}) %reduce-scatter.31.cloned.1.call-update) | async-done | bytes 124432
  (300 shorter events, 201.1 us)
Async XLA Ops:
  7.2 132.3 %copy-start.69 = (bf16[9]{0:T(256)(128)(2,1)S(1)}, bf16[9]{0:T(256)(128)(2,1)}, u32[]{:S(2)}) copy-start(bf16[9]{0:T(256)(128)(2,1)} %param.19) | copy-start | bytes 58
  7.2 132.5 %copy-start.70 = (bf16[9]{0:T(256)(128)(2,1)S(1)}, bf16[9]{0:T(256)(128)(2,1)}, u32[]{:S(2)}) copy-start(bf16[9]{0:T(256)(128)(2,1)} %param.24) | copy-start | bytes 58
  7.2 198.2 %copy-start.56 = (s32[1,512]{1,0:T(1,128)S(1)}, s32[1,512]{1,0:T(1,128)}, u32[]{:S(2)}) copy-start(s32[1,512]{1,0:T(1,128)} %param.18) | copy-start | bytes 6148
  7.3 198.3 %copy-start.3 = (bf16[1,128,1152]{2,1,0:T(8,128)(2,1)S(1)}, bf16[1,128,1152]{2,1,0:T(8,128)(2,1)}, u32[]{:S(2)}) copy-start(bf16[1,128,1152]{2,1,0:T(8,128)(2,1)} %param.16) | copy-start | bytes 884740
  7.3 225.0 %all-gather.14.cloned.1.call-start = ((), (), s32[]{:S(2)}) async-start(), calls=%async_computation.20 | async-start | bytes 4227072 | tf_op jit(solution)/shard_map/all_gather | solution.py:126
  8.0 236.8 %all-gather.12.cloned.1.call-start = ((), (), s32[]{:S(2)}) async-start(), calls=%async_computation.10 | async-start | bytes 2377728 | tf_op jit(solution)/shard_map/all_gather | solution.py:129
  8.7 241.1 %all-gather.16.cloned.1.call-start = ((), (), s32[]{:S(2)}) async-start(), calls=%async_computation.21 | async-start | bytes 28532736 | tf_op jit(solution)/shard_map/all_gather | solution.py:197
  9.5 340.8 %all-gather.18.cloned.1.call-start = ((), (), s32[]{:S(2)}) async-start(), calls=%async_computation.22 | async-start | bytes 28532736 | tf_op jit(solution)/shard_map/all_gather | solution.py:198
  10.1 422.0 %all-gather.20.cloned.1.call-start = ((), (), s32[]{:S(2)}) async-start(), calls=%async_computation.23 | async-start | bytes 16644096 | tf_op jit(solution)/shard_map/all_gather | solution.py:199
  10.6 643.6 %reduce-scatter.13.cloned.1.call-start = ((), (), s32[]{:S(2)}) async-start(), calls=%async_computation.11 | async-start | bytes 327680 | tf_op jit(solution)/shard_map/reduce_scatter | solution.py:299
  76.2 155.9 %copy-start.20 = (bf16[1152,256]{1,0:T(8,128)(2,1)}, bf16[1152,256]{1,0:T(8,128)(2,1)S(1)}, u32[]{:S(2)}) copy-start(bf16[1152,256]{1,0:T(8,128)(2,1)S(1)} %reshape.401) | copy-start | bytes 1769476
  248.4 132.5 %copy-start.12 = (bf16[128,1152]{1,0:T(8,128)(2,1)}, bf16[128,1152]{1,0:T(8,128)(2,1)S(1)}, u32[]{:S(2)}) copy-start(bf16[128,1152]{1,0:T(8,128)(2,1)S(1)} %multiply_convert_fusion.3) | copy-start | bytes 884740
  499.9 157.4 %reduce-scatter.15.cloned.1.call-start = ((), (), s32[]{:S(2)}) async-start(), calls=%async_computation.12 | async-start | bytes 327680 | tf_op jit(solution)/shard_map/reduce_scatter | solution.py:302
  502.2 190.6 %reduce-scatter.25.cloned.1.call-start = ((), (), s32[]{:S(2)}) async-start(), calls=%async_computation.17 | async-start | bytes 19906560 | tf_op jit(solution)/shard_map/reduce_scatter | solution.py:255
  552.0 284.5 %reduce-scatter.21.cloned.1.call-start = ((), (), s32[]{:S(2)}) async-start(), calls=%async_computation.15 | async-start | bytes 19906560 | tf_op jit(solution)/shard_map/reduce_scatter | solution.py:252
  601.7 378.3 %reduce-scatter.29.cloned.1.call-start = ((), (), s32[]{:S(2)}) async-start(), calls=%async_computation.19 | async-start | bytes 19906560 | tf_op jit(solution)/shard_map/reduce_scatter | solution.py:258
  644.5 356.2 %reduce-scatter.17.cloned.1.call-start = ((), (), s32[]{:S(2)}) async-start(), calls=%async_computation.13 | async-start | bytes 20480 | tf_op jit(solution)/shard_map/reduce_scatter | solution.py:246
  650.3 373.2 %reduce-scatter.19.cloned.1.call-start = ((), (), s32[]{:S(2)}) async-start(), calls=%async_computation.14 | async-start | bytes 20480 | tf_op jit(solution)/shard_map/reduce_scatter | solution.py:249
  654.2 569.7 %all-reduce.27.cloned.1.call-start = ((), (), s32[]{:S(2)}) async-start(), calls=%async_computation.25 | async-start | bytes 23592960
  659.6 629.2 %reduce-scatter.27.cloned.1.call-start = ((), (), s32[]{:S(2)}) async-start(), calls=%async_computation.18 | async-start | bytes 7299072 | tf_op jit(solution)/shard_map/reduce_scatter | solution.py:272
  700.1 680.1 %reduce-scatter.23.cloned.1.call-start = ((), (), s32[]{:S(2)}) async-start(), calls=%async_computation.16 | async-start | bytes 7299072 | tf_op jit(solution)/shard_map/reduce_scatter | solution.py:269
  843.9 621.3 %reduce-scatter.31.cloned.1.call-start = ((), (), s32[]{:S(2)}) async-start(), calls=%async_computation.24 | async-start | bytes 4257792
  987.1 235.7 %copy-start.64 = (f32[128]{0:T(128)S(1)}, f32[128]{0:T(128)}, u32[]{:S(2)}) copy-start(f32[128]{0:T(128)} %copy-done.63) | copy-start | bytes 1540
  987.1 235.8 %copy-start.18 = (f32[128,1152]{1,0:T(8,128)S(1)}, f32[128,1152]{1,0:T(8,128)}, u32[]{:S(2)}) copy-start(f32[128,1152]{1,0:T(8,128)} %copy-done.17) | copy-start | bytes 1769476
  (66 other events, 1078.0 us)
Sparse Core Ops, SparseCore 0:
  11.3 70.5 all-gather.13
  84.8 62.8 all-gather.11
  150.7 99.0 all-gather.15
  252.7 97.5 all-gather.17
  353.1 78.9 all-gather.19
  500.0 17.4 reduce-scatter.12
  520.0 20.2 reduce-scatter.14
  552.1 140.5 reduce-scatter.24
  695.4 141.1 reduce-scatter.20
  838.8 141.1 reduce-scatter.28
  983.0 17.6 reduce-scatter.16
  1003.5 19.9 reduce-scatter.18
  1030.0 170.1 all-reduce.26
  1204.3 84.4 reduce-scatter.26
  1292.9 87.1 reduce-scatter.22
  1384.2 80.9 reduce-scatter.30
where the time goes:
time: 1480 us; the launch traced here: 1470 us
  waiting for transfers between devices  699 us (47%)
  blocking collectives  409 us (28%)
  local copies, waits for them, and re-layouts  228 us (15%)
  matrix products  107 us (7%)
  between operations  15.3 us (1%)
    unnamed x3, blocking collectives  257 us
    reduce_scatter x1, waiting for transfers between devices, local(): lax.psum_scatter(owned[2].astype(jnp.bfloat16), 'ctx', scatter_dimension=...  136 us
    reduce_scatter x1, waiting for transfers between devices, local(): lax.psum_scatter(owned[4].astype(jnp.bfloat16), 'ctx', scatter_dimension=...  136 us
    reduce_scatter x1, waiting for transfers between devices, local(): lax.psum_scatter(within[2].astype(jnp.bfloat16), 'dp', scatter_dimension=...  89.6 us
    unnamed x174, local copies, waits for them, and re-layouts  86.8 us
    unnamed x18, waiting for transfers between devices  86.6 us
    all_gather x1, waiting for transfers between devices, local(): lax.all_gather(w_up, ('dp', 'ctx'), axis=0, tiled=True)  78.1 us
    all_gather x1, blocking collectives, local(): lax.all_gather(w_key, ('dp', 'ctx'), axis=0, tiled=True)  65.3 us
  transfers between devices with their start and end apart: 16, of which 11 were waited for; matrix products, arithmetic and copies ran while one was open for 18% of the time, Pallas kernels for 0%

commit v1 on v0

v1 whole, which is shorter than its diff:
```python
import math

import jax
import jax.numpy as jnp
from jax import lax
from jax.sharding import PartitionSpec as P

norm_eps = 1e-06
rope_base = 1000000.0
score_scale = 0.0625
far_below = -1e30
f32 = jnp.float32
bf16 = jnp.bfloat16
pack_rows = 16


def rms_norm(values, gain):
    factor = lax.rsqrt(jnp.mean(values * values, axis=-1, keepdims=True) + norm_eps)
    return values * factor * (1.0 + gain)


def rotate(values, cosine, sine):
    half_dim = values.shape[-1] // 2
    first_half = values[..., :half_dim]
    second_half = values[..., half_dim:]
    return jnp.concatenate(
        [first_half * cosine - second_half * sine, second_half * cosine + first_half * sine],
        axis=-1,
    )


def rope_tables(positions, head_dim):
    freq_index = jnp.arange(head_dim // 2, dtype=f32)
    inverse = jnp.exp(freq_index * (-2.0 / head_dim) * math.log(rope_base))
    angles = positions.astype(f32)[:, None] * inverse[None, :]
    return (jnp.cos(angles), jnp.sin(angles))


def gated_unit(gate_pre, up_pre):
    return jax.nn.gelu(gate_pre, approximate=True) * up_pre


def contract(left, right, left_dim, right_dim, kind=f32):
    return lax.dot_general(
        left, right, (((left_dim,), (right_dim,)), ((), ())), preferred_element_type=kind
    )


def from_ahead(block, step):
    size = lax.axis_size("ctx")
    return lax.ppermute(block, "ctx", [(i, (i - step) % size) for i in range(size)])


def to_ahead(block, step):
    size = lax.axis_size("ctx")
    return lax.ppermute(block, "ctx", [(i, (i + step) % size) for i in range(size)])


def gather_ahead(block):
    size = lax.axis_size("ctx")
    return jnp.concatenate([block] + [from_ahead(block, s) for s in range(1, size)], axis=0)


def sum_ahead(terms):
    arrived = [to_ahead(terms[s].astype(bf16), s) for s in range(1, len(terms))]
    total = terms[0].astype(f32)
    for item in arrived:
        total = total + item.astype(f32)
    return total


def swap_ctx(pieces):
    size = pieces.shape[0]
    me = lax.axis_index("ctx")
    result = jnp.zeros_like(pieces)
    own = lax.dynamic_index_in_dim(pieces, me, 0, keepdims=True)
    result = lax.dynamic_update_slice_in_dim(result, own, me, 0)
    for s in range(1, size):
        item = lax.dynamic_index_in_dim(pieces, (me + s) % size, 0, keepdims=True)
        item = to_ahead(item, s)
        result = lax.dynamic_update_slice_in_dim(result, item, (me - s) % size, 0)
    return result


def owner_pairs(outer, inner):
    return [(d, (d % outer) * inner + d // outer) for d in range(outer * inner)]


def local(
    activations,
    cotangent,
    segments,
    in_gain,
    query_gain,
    key_gain,
    post_attn_gain,
    pre_ff_gain,
    post_ff_gain,
    w_query,
    w_key,
    w_value,
    w_out,
    w_gate,
    w_up,
    w_down,
):
    outer = lax.axis_size("dp")
    inner = lax.axis_size("ctx")
    owners = outer * inner
    me = lax.axis_index("ctx")
    rows = w_query.shape[0]
    model = rows * owners
    qkv_cols = w_query.shape[1] + w_key.shape[1] + w_value.shape[1]
    query_cols = w_query.shape[1]
    head_dim = w_key.shape[1]
    heads = query_cols // head_dim
    out_rows = w_out.shape[0] * w_out.shape[1] // qkv_cols

    gains = (in_gain, query_gain, key_gain, post_attn_gain, pre_ff_gain, post_ff_gain)
    gain_row = jnp.concatenate(gains)
    gain_row = jnp.pad(gain_row, (0, qkv_cols - gain_row.shape[0]))[None]
    packed = jnp.concatenate(
        [
            jnp.concatenate([w_query, w_key, w_value], axis=1),
            w_out.reshape(out_rows, qkv_cols),
            gain_row,
        ],
        axis=0,
    )
    attn_all = lax.all_gather(packed, ("dp", "ctx"), axis=0, tiled=True)
    by_owner = attn_all.reshape(owners, pack_rows, qkv_cols)
    full_out = by_owner[:, rows : rows + out_rows, :].reshape(query_cols, model)
    gain_all = by_owner[:, pack_rows - 1, :128].astype(f32)
    full_gains = []
    first = 0
    for item in gains:
        size = item.shape[0]
        full_gains.append(gain_all[:, first : first + size].reshape(size * owners))
        first += size
    gain_in, gain_query, gain_key, gain_post_attn, gain_pre, gain_post = full_gains

    part = w_gate.shape[1] // inner
    both = jnp.concatenate(
        [w_gate.reshape(rows, inner, part), w_up.reshape(rows, inner, part)], axis=2
    ).transpose(1, 0, 2)
    both = swap_ctx(both).reshape(inner * rows, 2 * part)
    down_part = lax.ppermute(w_down, ("dp", "ctx"), owner_pairs(outer, inner))
    down_rows = w_down.shape[0] // 3
    ffn_packed = jnp.concatenate(
        [
            both,
            jnp.concatenate([down_part[i * down_rows : (i + 1) * down_rows] for i in range(3)], axis=1),
        ],
        axis=0,
    )
    ffn_all = lax.all_gather(ffn_packed, "dp", axis=0, tiled=False)
    full_both = ffn_all[:, : inner * rows, :].reshape(model, 2 * part)
    full_down = (
        ffn_all[:, inner * rows :, :]
        .reshape(outer, down_rows, 3, model)
        .transpose(0, 2, 1, 3)
        .reshape(part, model)
    )

    inputs = activations[0].astype(f32)
    segment_all = segments[0]
    tok_count = inputs.shape[0]
    first_place = me * tok_count
    place_rows = first_place + jnp.arange(tok_count, dtype=jnp.int32)
    segment_rows = lax.dynamic_slice_in_dim(segment_all, first_place, tok_count)
    earlier = jnp.sum((segment_all[None, :] < segment_rows[:, None]).astype(jnp.int32), axis=1)
    cosine, sine = rope_tables(place_rows - earlier, head_dim)
    length = segment_all.shape[0]
    key_places = (first_place + jnp.arange(length, dtype=jnp.int32)) % length
    key_segments = jnp.take(segment_all, key_places)
    allowed = (segment_rows[:, None] == key_segments[None, :]) & (
        place_rows[:, None] >= key_places[None, :]
    )
    allowed = jnp.tile(allowed, (heads, 1))

    model_index = jnp.arange(model, dtype=jnp.int32)
    padded_index = model_index // rows * pack_rows + model_index % rows
    spread = (
        padded_index[:, None] == jnp.arange(owners * pack_rows, dtype=jnp.int32)[None, :]
    ).astype(bf16)

    normed, in_pull = jax.vjp(rms_norm, inputs, gain_in)
    normed_wide = contract(normed.astype(bf16), spread, 1, 0, bf16)
    qkv = contract(normed_wide, attn_all, 1, 0)
    query_raw = qkv[:, :query_cols].reshape(tok_count, heads, head_dim)
    key_raw = qkv[:, query_cols : query_cols + head_dim]
    value_low = qkv[:, query_cols + head_dim :].astype(bf16)

    def prepare(query_in, key_in, query_scale, key_scale):
        rotated_query = rotate(
            rms_norm(query_in, query_scale), cosine[:, None, :], sine[:, None, :]
        )
        rotated_key = rotate(rms_norm(key_in, key_scale), cosine, sine)
        return (rotated_query, rotated_key)

    (queries, key_rows), prepare_pull = jax.vjp(prepare, query_raw, key_raw, gain_query, gain_key)
    query_low = queries.astype(bf16).transpose(1, 0, 2).reshape(heads * tok_count, head_dim)
    key_value = gather_ahead(jnp.concatenate([key_rows.astype(bf16), value_low], axis=1))
    key_all = key_value[:, :head_dim]
    value_all = key_value[:, head_dim:]

    scores = contract(query_low, key_all, 1, 1) * score_scale
    scores = jnp.where(allowed, scores, far_below)
    top_score = jnp.max(scores, axis=-1, keepdims=True)
    weight = jnp.exp(scores - top_score)
    prob = weight / jnp.sum(weight, axis=-1, keepdims=True)
    prob_low = prob.astype(bf16)
    attended = contract(prob_low, value_all, 1, 0).astype(bf16)
    attended_low = attended.reshape(heads, tok_count, head_dim).transpose(1, 0, 2)
    attended_low = attended_low.reshape(tok_count, query_cols)
    attn_out = contract(attended_low, full_out, 1, 0)
    post_attn, post_attn_pull = jax.vjp(rms_norm, attn_out, gain_post_attn)
    middle = inputs + post_attn
    normed_ff, pre_pull = jax.vjp(rms_norm, middle, gain_pre)
    normed_all = gather_ahead(normed_ff.astype(bf16))

    gate_up = contract(normed_all, full_both, 1, 0)
    mixed, gated_pull = jax.vjp(gated_unit, gate_up[:, :part], gate_up[:, part:])
    mixed_low = mixed.astype(bf16)
    branch_term = contract(mixed_low, full_down, 1, 0)
    branch_out = sum_ahead(
        [branch_term[s * tok_count : (s + 1) * tok_count] for s in range(inner)]
    )
    post_ff, post_pull = jax.vjp(rms_norm, branch_out, gain_post)
    output = (middle + post_ff).astype(bf16)

    grad_output = cotangent[0].astype(f32)
    grad_branch, grad_post_ff = post_pull(grad_output)
    grad_branch_all = gather_ahead(grad_branch.astype(bf16))
    down_term = contract(mixed_low, grad_branch_all, 0, 0, bf16)
    grad_mixed = contract(grad_branch_all, full_down, 1, 1)
    grad_gate, grad_up = gated_pull(grad_mixed)
    grad_both = jnp.concatenate([grad_gate.astype(bf16), grad_up.astype(bf16)], axis=1)
    both_term = contract(normed_all, grad_both, 0, 0, bf16)
    grad_normed_term = contract(grad_both, full_both, 1, 1)
    ffn_terms = jnp.concatenate(
        [
            both_term.reshape(outer, inner * rows, 2 * part),
            down_term.reshape(outer, 3, down_rows, model)
            .transpose(0, 2, 1, 3)
            .reshape(outer, down_rows, 2 * part),
            jnp.zeros((outer, -(inner * rows + down_rows) % 64, 2 * part), bf16),
        ],
        axis=1,
    )
    ffn_sum = lax.psum_scatter(
        ffn_terms.reshape(-1, 2 * part), "dp", scatter_dimension=0, tiled=True
    )
    both_grad = swap_ctx(ffn_sum[: inner * rows].reshape(inner, rows, 2 * part))
    both_grad = both_grad.astype(f32).transpose(1, 0, 2)
    gate_grad = both_grad[:, :, :part].reshape(rows, inner * part)
    up_grad = both_grad[:, :, part:].reshape(rows, inner * part)
    down_grad = jnp.concatenate(
        [
            ffn_sum[inner * rows : inner * rows + down_rows, i * model : (i + 1) * model]
            for i in range(3)
        ], axis=0
    )
    down_grad = lax.ppermute(
        down_grad, ("dp", "ctx"), [(b, a) for a, b in owner_pairs(outer, inner)]
    ).astype(f32)

    grad_normed_ff = sum_ahead(
        [grad_normed_term[s * tok_count : (s + 1) * tok_count] for s in range(inner)]
    )
    grad_middle_add, grad_pre_ff = pre_pull(grad_normed_ff)
    grad_middle = grad_output + grad_middle_add
    grad_attn, grad_post_attn = post_attn_pull(grad_middle)
    grad_attn_low = grad_attn.astype(bf16)
    out_term = contract(attended_low, grad_attn_low, 0, 0, bf16)
    grad_attended = contract(grad_attn_low, full_out, 1, 1, bf16)
    grad_attended = grad_attended.reshape(tok_count, heads, head_dim).transpose(1, 0, 2)
    grad_attended = grad_attended.reshape(heads * tok_count, head_dim)

    grad_prob = contract(grad_attended, value_all, 1, 1)
    shift_term = jnp.sum(prob * grad_prob, axis=-1, keepdims=True)
    grad_scores = (prob * (grad_prob - shift_term)).astype(bf16)
    grad_query = contract(grad_scores, key_all, 1, 0) * score_scale
    grad_key = contract(grad_scores, query_low, 0, 0) * score_scale
    grad_value = contract(prob_low, grad_attended, 0, 0)
    grad_key_value = jnp.concatenate([grad_key, grad_value], axis=1)
    grad_key_value = sum_ahead(
        [grad_key_value[s * tok_count : (s + 1) * tok_count] for s in range(inner)]
    )
    grad_queries = grad_query.reshape(heads, tok_count, head_dim).transpose(1, 0, 2)
    grad_query_raw, grad_key_raw, grad_query_gain, grad_key_gain = prepare_pull(
        (grad_queries, grad_key_value[:, :head_dim])
    )
    grad_qkv = jnp.concatenate(
        [
            grad_query_raw.reshape(tok_count, query_cols),
            grad_key_raw,
            grad_key_value[:, head_dim:],
        ],
        axis=1,
    ).astype(bf16)
    qkv_term = contract(normed_wide, grad_qkv, 0, 0, bf16)
    grad_normed_wide = contract(grad_qkv, attn_all, 1, 1, bf16)
    grad_normed = contract(grad_normed_wide, spread, 1, 1)
    grad_input_add, grad_in_gain = in_pull(grad_normed)
    input_grad = grad_middle + grad_input_add

    grad_gains = (
        grad_in_gain,
        grad_query_gain,
        grad_key_gain,
        grad_post_attn,
        grad_pre_ff,
        grad_post_ff,
    )
    gain_terms = jnp.concatenate([item.reshape(owners, -1) for item in grad_gains], axis=1)
    gain_terms = jnp.pad(gain_terms, ((0, 0), (0, qkv_cols - gain_terms.shape[1])))
    attn_terms = jnp.concatenate(
        [
            qkv_term.reshape(owners, pack_rows, qkv_cols)[:, :rows],
            out_term.reshape(owners, out_rows, qkv_cols),
            gain_terms[:, None].astype(bf16),
        ],
        axis=1,
    ).reshape(outer, inner, pack_rows, qkv_cols)
    attn_sum = lax.psum_scatter(attn_terms, "dp", scatter_dimension=0, tiled=False)
    attn_swapped = swap_ctx(attn_sum).astype(f32)
    attn_grad = jnp.sum(attn_swapped, axis=0)
    gain_grads = []
    first = 0
    for item in gains:
        size = item.shape[0]
        gain_grads.append(attn_grad[pack_rows - 1, first : first + size])
        first += size
    return (
        output[None],
        input_grad[None],
        *gain_grads,
        attn_grad[:rows, :query_cols],
        attn_grad[:rows, query_cols : query_cols + head_dim],
        attn_grad[:rows, query_cols + head_dim :],
        attn_grad[rows : rows + out_rows].reshape(w_out.shape),
        gate_grad,
        up_grad,
        down_grad,
    )


def solution(mesh):
    shard = P(("dp", "ctx"))
    matrix = P(("dp", "ctx"), None)
    tokens = P("dp", "ctx", None)
    return jax.shard_map(
        local,
        mesh=mesh,
        in_specs=(tokens, tokens, P("dp", None)) + (shard,) * 6 + (matrix,) * 7,
        out_specs=(tokens, tokens) + (shard,) * 6 + (matrix,) * 7,
        check_vma=False,
    )
```

time: 1480 us -> 582 us (0.39)
  waiting for transfers between devices: 699 us -> 234 us
  blocking collectives: 409 us -> 0 us
  local copies, waits for them, and re-layouts: 228 us -> 150 us
  starting transfers between devices: 1.26 us -> 50.3 us
  matrix products: 107 us -> 67.2 us
  other arithmetic: 14.2 us -> 53.1 us
    reduce_scatter x9 -> x2, waiting for transfers between devices: 490 us -> 117 us  [the longest x1 101 us: local(): lax.psum_scatter(ffn_terms.reshape(-1, 2 * part), 'dp', scatter_dimension...]
    unnamed x3 -> x0, blocking collectives: 257 us -> none
    all_gather x4 -> x0, blocking collectives: 151 us -> none  [the longest x1 65.3 us: local(): lax.all_gather(w_key, ('dp', 'ctx'), axis=0, tiled=True)]
    convert_element_type x11 -> x0, local copies, waits for them, and re-layouts: 117 us -> none  [the longest x2 40.4 us: local(): owned[3].astype(jnp.bfloat16)]
    unnamed x18 -> x4, waiting for transfers between devices: 86.6 us -> 0.07 us
    reshape x0 -> x30, local copies, waits for them, and re-layouts: none -> 80.4 us  [the longest x2 17.4 us: local(): ffn_terms = jnp.concatenate([both_term.reshape(outer, inner * rows, 2 * p...]
    unnamed x174 -> x166, local copies, waits for them, and re-layouts: 86.8 us -> 9.85 us
    all_gather x5 -> x2, waiting for transfers between devices: 123 us -> 70.5 us  [the longest x1 46.2 us: local(): attn_all = lax.all_gather(packed, ('dp', 'ctx'), axis=0, tiled=True)]
  transfers between devices with their start and end apart: 16 -> 33, of which waited for: 11 -> 15; matrix products, arithmetic and copies ran while one was open for 18% -> 31% of each run, Pallas kernels for 0% -> 0%
where the time goes in v1:
time: 582 us; the launch traced here: 571 us
  waiting for transfers between devices  234 us (40%)
  local copies, waits for them, and re-layouts  150 us (26%)
  matrix products  67.2 us (12%)
  other arithmetic  53.1 us (9%)
  starting transfers between devices  50.3 us (9%)
  between operations  15.6 us (3%)
    reduce_scatter x1, waiting for transfers between devices, local(): lax.psum_scatter(ffn_terms.reshape(-1, 2 * part), 'dp', scatter_dimension...  101 us
    dot_general x19, matrix products, contract(): lax.dot_general(left, right, (((left_dim,), (right_dim,)), ((), ())), pre...  67.2 us
    all_gather x1, waiting for transfers between devices, local(): attn_all = lax.all_gather(packed, ('dp', 'ctx'), axis=0, tiled=True)  46.2 us
    ppermute x18, waiting for transfers between devices, to_ahead(): lax.ppermute(block, 'ctx', [(i, (i + step) % size) for i in range(size)])  34 us
    ppermute x18, starting transfers between devices, to_ahead(): lax.ppermute(block, 'ctx', [(i, (i + step) % size) for i in range(size)])  27.2 us
    all_gather x1, waiting for transfers between devices, local(): ffn_all = lax.all_gather(ffn_packed, 'dp', axis=0, tiled=False)  24.3 us
    reshape x2, local copies, waits for them, and re-layouts, local(): ffn_terms = jnp.concatenate([both_term.reshape(outer, inner * rows, 2 * p...  17.4 us
    reshape x2, local copies, waits for them, and re-layouts, local(): full_down = ffn_all[:, inner * rows:, :].reshape(outer, down_rows, 3, mod...  16.1 us
  transfers between devices with their start and end apart: 33, of which 15 were waited for; matrix products, arithmetic and copies ran while one was open for 31% of the time, Pallas kernels for 0%

profile of v1, /device:TPU:1, one launch (start us, length us, event | category | flops | bytes accessed | tf_op | source)
XLA Modules:
  0.0 570.6 jit_solution(17981785915756936921)
XLA Ops:
  13.6 6.9 %collective-permute-start.9 = (bf16[54,1152]{1,0:T(8,128)(2,1)}, bf16[54,1152]{1,0:T(8,128)(2,1)S(1)}, u32[]{:S(2)}, u32[]{:S(2)}) collective-permute-start(bf16[54,1152]{1,0:T(8,128)(2,1)} %param.31), channel_id=1, source_target_pairs={{0,0},{1,4},{2,8},{3,12},{4,16},{5,20},{6,24},{7,28},{8,32},{9,36}... | collective-permute-start | bytes 373256 | tf_op jit(solution)/shard_map/ppermute | solution.py:147
  40.4 46.2 %all-gather.5.cloned.1.call-done = bf16[2048,1536]{1,0:T(8,128)(2,1)} async-done(((bf16[16,1536]{1,0:T(8,128)(2,1)}), bf16[2048,1536]{1,0:T(8,128)(2,1)}) %all-gather.5.cloned.1.call-update) | async-done | bytes 6291472 | tf_op jit(solution)/shard_map/all_gather | solution.py:130
  125.4 24.3 %all-gather.7.cloned.1.call-done = bf16[32,54,3456]{2,1,0:T(8,128)(2,1)} async-done(((bf16[1,54,3456]{2,1,0:T(8,128)(2,1)}), bf16[32,54,3456]{2,1,0:T(8,128)(2,1)}) %all-gather.7.cloned.1.call-update) | async-done | bytes 11943952 | tf_op jit(solution)/shard_map/all_gather | solution.py:156
  156.5 7.5 %slice.251 = bf16[32,36,3456]{2,1,0:T(8,128)(2,1)} slice(bf16[32,54,3456]{2,1,0:T(8,128)(2,1)} %all-gather.7.cloned.1.call-done), slice={[0:32], [0:36], [0:3456]} | slice | bytes 15925248 | tf_op jit(solution)/shard_map/slice | solution.py:157
  164.0 13.0 %reshape.557 = bf16[1152,3456]{1,0:T(8,128)(2,1)} reshape(bf16[32,36,3456]{2,1,0:T(8,128)(2,1)} %slice.251) | data formatting | bytes 15925248 | tf_op jit(solution)/shard_map/reshape | solution.py:157
  177.0 8.8 %reshape.558 = bf16[32,18,3,1152]{3,2,0,1:T(4,128)(2,1)} reshape(bf16[32,18,3456]{2,0,1:T(8,128)(2,1)} %copy.158) | data formatting | bytes 7962624 | tf_op jit(solution)/shard_map/reshape | solution.py:160
  185.8 8.5 %copy.159 = bf16[32,3,18,1152]{3,2,1,0:T(8,128)(2,1)} copy(bf16[32,3,18,1152]{3,1,0,2:T(4,128)(2,1)} %bitcast.134) | data formatting | bytes 7962624 | tf_op jit(solution)/shard_map/transpose | solution.py:161
  194.3 7.3 %reshape.559 = bf16[1728,1152]{1,0:T(8,128)(2,1)} reshape(bf16[32,3,18,1152]{3,2,1,0:T(8,128)(2,1)} %copy.159) | data formatting | bytes 7962624 | tf_op jit(solution)/shard_map/reshape | solution.py:162
  201.6 7.7 %fusion.61 = f32[512,3456]{1,0:T(8,128)S(1)} fusion(bf16[1152,3456]{1,0:T(8,128)(2,1)} %reshape.557, bf16[128,1152]{1,0:T(8,128)(2,1)} %collective-permute-done.5, bf16[128,1152]{1,0:T(8,128)(2,1)} %collective-permute-done.4, bf16[128,1152]{1,0:T(8,128)(2,1)} %collective-permute-done.3, bf16[128,1152]{1,0:T(8,128)(2,1)S(1)} %multiply_convert_fusion.3), kind=kOutput, calls=%fused_computation.131 | convolution fusion | flops 4081582080 | bytes 16220160 | tf_op jit(solution)/shard_map/dot_general | solution.py:44
  228.7 7.3 %collective-permute-done.11 = bf16[128,1152]{1,0:T(8,128)(2,1)} collective-permute-done((bf16[128,1152]{1,0:T(8,128)(2,1)}, bf16[128,1152]{1,0:T(8,128)(2,1)}, u32[]{:S(2)}, u32[]{:S(2)}) %collective-permute-start.11) | collective-permute-done | bytes 294944 | tf_op jit(solution)/shard_map/ppermute | solution.py:56
  243.6 6.6 %collective-permute-done.15 = bf16[128,1152]{1,0:T(8,128)(2,1)S(1)} collective-permute-done((bf16[128,1152]{1,0:T(8,128)(2,1)S(1)}, bf16[128,1152]{1,0:T(8,128)(2,1)S(1)}, u32[]{:S(2)}, u32[]{:S(2)}) %collective-permute-start.15) | collective-permute-done | bytes 294944 | tf_op jit(solution)/shard_map/ppermute | solution.py:51
  256.6 7.3 %fusion.10 = (bf16[512,1728]{1,0:T(8,128)(2,1)S(1)}, bf16[512,1728]{1,0:T(8,128)(2,1)S(1)}) fusion(f32[512,3456]{1,0:T(8,128)} %copy-done.7, bf16[1728,1152]{1,0:T(8,128)(2,1)S(1)} %copy-done.16, bf16[128,1152]{1,0:T(8,128)(2,1)S(1)} %collective-permute-done.15, bf16[128,1152]{1,0:T(8,128)(2,1)S(1)} %collective-permute-done.14, ...), kind=kOutput, calls=%fused_computation.16 | convolution fusion | flops 2064384000 | bytes 15777792 | tf_op jit(solution)/shard_map/dot_general | solution.py:44
  264.0 6.3 %fusion.121 = (bf16[512,1152]{1,0:T(8,128)(2,1)S(1)}, f32[512,1152]{1,0:T(8,128)}) fusion(bf16[1152,3456]{1,0:T(8,128)(2,1)S(1)} %bitcast.140, bf16[512,1728]{1,0:T(8,128)(2,1)S(1)} %get-tuple-element.34, bf16[512,1728]{1,0:T(8,128)(2,1)S(1)} %get-tuple-element.33), kind=kOutput, calls=%fused_computation.263 | convolution fusion | flops 4084531200 | bytes 15040512 | tf_op jit(solution)/shard_map/dot_general | solution.py:44
  281.2 7.9 %collective-permute-done.17 = bf16[128,1152]{1,0:T(8,128)(2,1)} collective-permute-done((bf16[128,1152]{1,0:T(8,128)(2,1)}, bf16[128,1152]{1,0:T(8,128)(2,1)}, u32[]{:S(2)}, u32[]{:S(2)}) %collective-permute-start.17) | collective-permute-done | bytes 294944 | tf_op jit(solution)/shard_map/ppermute | solution.py:56
  320.7 7.8 %fusion.24 = (bf16[1152]{0:T(1024)(128)(2,1)S(1)}, f32[128]{0:T(128)S(1)}, f32[128,1152]{1,0:T(8,128)}) fusion(bf16[1,128,1152]{2,1,0:T(8,128)(2,1)S(1)} %copy-done.19, f32[128]{0:T(128)S(1)} %copy-done.64, f32[1152]{0:T(1024)S(1)} %copy-done.40, s32[1152]{0:T(1024)S(1)} %copy-done.49, bf16[2048,1536]{1,0:T(8,128)(2,1)} %all-gather.5.cloned.1.call-done, ...), kind=kOutput, calls=%fused_computation.59 | convolution fusion | flops 1413856000 | bytes 7581952 | tf_op jit(solution)/shard_map/dot_general | solution.py:44
  333.9 8.9 %pad_maximum_fusion = bf16[32,4,16,1536]{3,2,1,0:T(8,128)(2,1)} fusion(bf16[32,4,1,1536]{3,2,1,0:T(2,128)(2,1)} %concatenate.88, bf16[32,4,6,1536]{3,2,1,0:T(8,128)(2,1)S(1)} %concatenate.82, bf16[32,4,9,1536]{3,2,1,0:T(8,128)(2,1)} %bitcast.131), kind=kLoop, calls=%fused_computation.5 | loop fusion | flops 18874368 | bytes 12582912 | tf_op jit(solution)/shard_map/concatenate | solution.py:318
  349.0 7.2 %reshape.572 = bf16[32,3,18,1152]{3,2,1,0:T(8,128)(2,1)} reshape(bf16[1728,1152]{1,0:T(8,128)(2,1)} %fusion.59) | data formatting | bytes 7962624 | tf_op jit(solution)/shard_map/reshape | solution.py:244
  356.1 7.1 %copy.184 = bf16[32,18,3,1152]{3,2,1,0:T(4,128)(2,1)} copy(bf16[32,18,3,1152]{3,1,2,0:T(8,128)(2,1)} %bitcast.135) | data formatting | bytes 7962624 | tf_op jit(solution)/shard_map/reshape | solution.py:246
  363.3 10.3 %reshape.594 = bf16[32,18,3456]{2,1,0:T(8,128)(2,1)} reshape(bf16[32,18,3,1152]{3,2,1,0:T(4,128)(2,1)} %copy.184) | data formatting | bytes 7962624 | tf_op jit(solution)/shard_map/reshape | solution.py:246
  373.6 9.6 %fusion.11 = bf16[1152,3456]{1,0:T(8,128)(2,1)} fusion(bf16[512,1728]{1,0:T(8,128)(2,1)} %copy-done.78, bf16[512,1728]{1,0:T(8,128)(2,1)S(1)} %copy-done.77, bf16[128,1152]{1,0:T(8,128)(2,1)} %collective-permute-done.5, bf16[128,1152]{1,0:T(8,128)(2,1)} %collective-permute-done.4, bf16[128,1152]{1,0:T(8,128)(2,1)} %collective-permute-done.3, ...), kind=kOutput, calls=%fused_computation.21 | convolution fusion | flops 4088659968 | bytes 12681216 | tf_op jit(solution)/shard_map/dot_general | solution.py:44
  383.1 12.5 %reshape.571 = bf16[32,36,3456]{2,1,0:T(8,128)(2,1)} reshape(bf16[1152,3456]{1,0:T(8,128)(2,1)} %fusion.11) | data formatting | bytes 15925248 | tf_op jit(solution)/shard_map/reshape | solution.py:243
  395.6 15.1 %maximum_maximum_fusion = bf16[32,64,3456]{2,1,0:T(8,128)(2,1)} fusion(bf16[32,18,3456]{2,1,0:T(8,128)(2,1)} %reshape.594, bf16[32,36,3456]{2,1,0:T(8,128)(2,1)} %reshape.571, bf16[64]{0:T(256)(128)(2,1)S(1)} %pad.32.clone), kind=kLoop, calls=%fused_computation.1 | loop fusion | flops 42467328 | bytes 26099840 | tf_op jit(solution)/shard_map/concatenate | solution.py:241
  413.0 15.8 %reduce-scatter.3.cloned.1.call-done = bf16[1,4,16,1536]{3,2,1,0:T(8,128)(2,1)} async-done(((bf16[32,4,16,1536]{3,2,1,0:T(8,128)(2,1)}), bf16[1,4,16,1536]{3,2,1,0:T(8,128)(2,1)}) %reduce-scatter.3.cloned.1.call-update) | async-done | bytes 196624 | tf_op jit(solution)/shard_map/reduce_scatter | solution.py:326
  440.3 101.1 %reduce-scatter.5.cloned.1.call-done = bf16[64,3456]{1,0:T(8,128)(2,1)} async-done(((bf16[2048,3456]{1,0:T(8,128)(2,1)}), bf16[64,3456]{1,0:T(8,128)(2,1)}) %reduce-scatter.5.cloned.1.call-update) | async-done | bytes 442384 | tf_op jit(solution)/shard_map/reduce_scatter | solution.py:251
  (386 shorter events, 194.3 us)
Async XLA Ops:
  7.2 79.4 %all-gather.5.cloned.1.call-start = ((), (), s32[]{:S(2)}) async-start(), calls=%async_computation.2 | async-start | bytes 6340608 | tf_op jit(solution)/shard_map/all_gather | solution.py:130
  13.6 136.1 %all-gather.7.cloned.1.call-start = ((), (), s32[]{:S(2)}) async-start(), calls=%async_computation.5 | async-start | bytes 12773376 | tf_op jit(solution)/shard_map/all_gather | solution.py:156
  13.6 20.5 %collective-permute-start.9 = (bf16[54,1152]{1,0:T(8,128)(2,1)}, bf16[54,1152]{1,0:T(8,128)(2,1)S(1)}, u32[]{:S(2)}, u32[]{:S(2)}) collective-permute-start(bf16[54,1152]{1,0:T(8,128)(2,1)} %param.31), channel_id=1, source_target_pairs={{0,0},{1,4},{2,8},{3,12},{4,16},{5,20},{6,24},{7,28},{8,32},{9,36}... | collective-permute-start | bytes 373256 | tf_op jit(solution)/shard_map/ppermute | solution.py:147
  23.7 9.3 %collective-permute-start.7 = (bf16[1,9,3456]{2,1,0:T(8,128)(2,1)S(1)}, bf16[1,9,3456]{2,1,0:T(8,128)(2,1)S(1)}, u32[]{:S(2)}, u32[]{:S(2)}) collective-permute-start(bf16[1,9,3456]{2,1,0:T(8,128)(2,1)S(1)} %bitcast.154), channel_id=1, source_target_pairs={{0,2},{1,3},{2,0},{3,1},{4,6},{5,7},{6,4},{7,5},{8,10},{9,11},{10,... | collective-permute-start | bytes 186632 | tf_op jit(solution)/shard_map/ppermute | solution.py:56
  35.0 393.8 %reduce-scatter.3.cloned.1.call-start = ((), (), s32[]{:S(2)}) async-start(), calls=%async_computation.3 | async-start | bytes 6488064 | tf_op jit(solution)/shard_map/reduce_scatter | solution.py:326
  96.5 14.2 %collective-permute-start.2 = (bf16[128,512]{1,0:T(8,128)(2,1)}, bf16[128,512]{1,0:T(8,128)(2,1)}, u32[]{:S(2)}, u32[]{:S(2)}) collective-permute-start(bf16[128,512]{1,0:T(8,128)(2,1)} %pad_maximum_fusion.17), channel_id=1, source_target_pairs={{0,1},{1,2},{2,3},{3,0},{4,5},{5,6},{6,7},{7,4},{8,9},{9,10},{10,1... | collective-permute-start | bytes 393224 | tf_op jit(solution)/shard_map/ppermute | solution.py:51
  96.5 14.2 %collective-permute-start.1 = (bf16[128,512]{1,0:T(8,128)(2,1)}, bf16[128,512]{1,0:T(8,128)(2,1)}, u32[]{:S(2)}, u32[]{:S(2)}) collective-permute-start(bf16[128,512]{1,0:T(8,128)(2,1)} %pad_maximum_fusion.17), channel_id=1, source_target_pairs={{0,2},{1,3},{2,0},{3,1},{4,6},{5,7},{6,4},{7,5},{8,10},{9,11},{10,... | collective-permute-start | bytes 393224 | tf_op jit(solution)/shard_map/ppermute | solution.py:51
  98.5 12.2 %collective-permute-start = (bf16[128,512]{1,0:T(8,128)(2,1)}, bf16[128,512]{1,0:T(8,128)(2,1)}, u32[]{:S(2)}, u32[]{:S(2)}) collective-permute-start(bf16[128,512]{1,0:T(8,128)(2,1)} %pad_maximum_fusion.17), channel_id=1, source_target_pairs={{0,3},{1,0},{2,1},{3,2},{4,7},{5,4},{6,5},{7,6},{8,11},{9,8},{10,9... | collective-permute-start | bytes 393224 | tf_op jit(solution)/shard_map/ppermute | solution.py:51
  121.4 80.1 %collective-permute-start.5 = (bf16[128,1152]{1,0:T(8,128)(2,1)S(1)}, bf16[128,1152]{1,0:T(8,128)(2,1)}, u32[]{:S(2)}, u32[]{:S(2)}) collective-permute-start(bf16[128,1152]{1,0:T(8,128)(2,1)S(1)} %multiply_convert_fusion.3), channel_id=1, source_target_pairs={{0,1},{1,2},{2,3},{3,0},{4,5},{5,6},{6,7},{7,4},{8,9},{9,10},{10,1... | collective-permute-start | bytes 884744 | tf_op jit(solution)/shard_map/ppermute | solution.py:51
  121.7 79.8 %collective-permute-start.4 = (bf16[128,1152]{1,0:T(8,128)(2,1)S(1)}, bf16[128,1152]{1,0:T(8,128)(2,1)}, u32[]{:S(2)}, u32[]{:S(2)}) collective-permute-start(bf16[128,1152]{1,0:T(8,128)(2,1)S(1)} %multiply_convert_fusion.3), channel_id=1, source_target_pairs={{0,2},{1,3},{2,0},{3,1},{4,6},{5,7},{6,4},{7,5},{8,10},{9,11},{10,... | collective-permute-start | bytes 884744 | tf_op jit(solution)/shard_map/ppermute | solution.py:51
  123.4 78.2 %collective-permute-start.3 = (bf16[128,1152]{1,0:T(8,128)(2,1)S(1)}, bf16[128,1152]{1,0:T(8,128)(2,1)}, u32[]{:S(2)}, u32[]{:S(2)}) collective-permute-start(bf16[128,1152]{1,0:T(8,128)(2,1)S(1)} %multiply_convert_fusion.3), channel_id=1, source_target_pairs={{0,3},{1,0},{2,1},{3,2},{4,7},{5,4},{6,5},{7,6},{8,11},{9,8},{10,9... | collective-permute-start | bytes 884744 | tf_op jit(solution)/shard_map/ppermute | solution.py:51
  218.8 9.9 %collective-permute-start.10 = (bf16[128,1152]{1,0:T(8,128)(2,1)}, bf16[128,1152]{1,0:T(8,128)(2,1)}, u32[]{:S(2)}, u32[]{:S(2)}) collective-permute-start(bf16[128,1152]{1,0:T(8,128)(2,1)} %get-tuple-element.38), channel_id=1, source_target_pairs={{0,1},{1,2},{2,3},{3,0},{4,5},{5,6},{6,7},{7,4},{8,9},{9,10},{10,1... | collective-permute-start | bytes 884744 | tf_op jit(solution)/shard_map/ppermute | solution.py:56
  220.0 8.7 %collective-permute-start.12 = (bf16[128,1152]{1,0:T(8,128)(2,1)}, bf16[128,1152]{1,0:T(8,128)(2,1)}, u32[]{:S(2)}, u32[]{:S(2)}) collective-permute-start(bf16[128,1152]{1,0:T(8,128)(2,1)} %get-tuple-element.39), channel_id=1, source_target_pairs={{0,3},{1,0},{2,1},{3,2},{4,7},{5,4},{6,5},{7,6},{8,11},{9,8},{10,9... | collective-permute-start | bytes 884744 | tf_op jit(solution)/shard_map/ppermute | solution.py:56
  221.5 14.5 %collective-permute-start.11 = (bf16[128,1152]{1,0:T(8,128)(2,1)}, bf16[128,1152]{1,0:T(8,128)(2,1)}, u32[]{:S(2)}, u32[]{:S(2)}) collective-permute-start(bf16[128,1152]{1,0:T(8,128)(2,1)} %get-tuple-element.40), channel_id=1, source_target_pairs={{0,2},{1,3},{2,0},{3,1},{4,6},{5,7},{6,4},{7,5},{8,10},{9,11},{10,... | collective-permute-start | bytes 884744 | tf_op jit(solution)/shard_map/ppermute | solution.py:56
  240.4 9.7 %collective-permute-start.15 = (bf16[128,1152]{1,0:T(8,128)(2,1)S(1)}, bf16[128,1152]{1,0:T(8,128)(2,1)S(1)}, u32[]{:S(2)}, u32[]{:S(2)}) collective-permute-start(bf16[128,1152]{1,0:T(8,128)(2,1)S(1)} %get-tuple-element.47), channel_id=1, source_target_pairs={{0,1},{1,2},{2,3},{3,0},{4,5},{5,6},{6,7},{7,4},{8,9},{9,10},{10,1... | collective-permute-start | bytes 884744 | tf_op jit(solution)/shard_map/ppermute | solution.py:51
  241.1 13.5 %collective-permute-start.14 = (bf16[128,1152]{1,0:T(8,128)(2,1)S(1)}, bf16[128,1152]{1,0:T(8,128)(2,1)S(1)}, u32[]{:S(2)}, u32[]{:S(2)}) collective-permute-start(bf16[128,1152]{1,0:T(8,128)(2,1)S(1)} %get-tuple-element.47), channel_id=1, source_target_pairs={{0,2},{1,3},{2,0},{3,1},{4,6},{5,7},{6,4},{7,5},{8,10},{9,11},{10,... | collective-permute-start | bytes 884744 | tf_op jit(solution)/shard_map/ppermute | solution.py:51
  242.9 13.7 %collective-permute-start.13 = (bf16[128,1152]{1,0:T(8,128)(2,1)S(1)}, bf16[128,1152]{1,0:T(8,128)(2,1)S(1)}, u32[]{:S(2)}, u32[]{:S(2)}) collective-permute-start(bf16[128,1152]{1,0:T(8,128)(2,1)S(1)} %get-tuple-element.47), channel_id=1, source_target_pairs={{0,3},{1,0},{2,1},{3,2},{4,7},{5,4},{6,5},{7,6},{8,11},{9,8},{10,9... | collective-permute-start | bytes 884744 | tf_op jit(solution)/shard_map/ppermute | solution.py:51
  271.2 10.0 %collective-permute-start.16 = (bf16[128,1152]{1,0:T(8,128)(2,1)}, bf16[128,1152]{1,0:T(8,128)(2,1)}, u32[]{:S(2)}, u32[]{:S(2)}) collective-permute-start(bf16[128,1152]{1,0:T(8,128)(2,1)} %get-tuple-element.35), channel_id=1, source_target_pairs={{0,1},{1,2},{2,3},{3,0},{4,5},{5,6},{6,7},{7,4},{8,9},{9,10},{10,1... | collective-permute-start | bytes 884744 | tf_op jit(solution)/shard_map/ppermute | solution.py:56
  274.6 14.4 %collective-permute-start.17 = (bf16[128,1152]{1,0:T(8,128)(2,1)}, bf16[128,1152]{1,0:T(8,128)(2,1)}, u32[]{:S(2)}, u32[]{:S(2)}) collective-permute-start(bf16[128,1152]{1,0:T(8,128)(2,1)} %get-tuple-element.37), channel_id=1, source_target_pairs={{0,2},{1,3},{2,0},{3,1},{4,6},{5,7},{6,4},{7,5},{8,10},{9,11},{10,... | collective-permute-start | bytes 884744 | tf_op jit(solution)/shard_map/ppermute | solution.py:56
  300.3 8.8 %collective-permute-start.19 = (bf16[128,512]{1,0:T(8,128)(2,1)S(1)}, bf16[128,512]{1,0:T(8,128)(2,1)}, u32[]{:S(2)}, u32[]{:S(2)}) collective-permute-start(bf16[128,512]{1,0:T(8,128)(2,1)S(1)} %get-tuple-element.49), channel_id=1, source_target_pairs={{0,1},{1,2},{2,3},{3,0},{4,5},{5,6},{6,7},{7,4},{8,9},{9,10},{10,1... | collective-permute-start | bytes 393224 | tf_op jit(solution)/shard_map/ppermute | solution.py:56
  342.8 198.6 %reduce-scatter.5.cloned.1.call-start = ((), (), s32[]{:S(2)}) async-start(), calls=%async_computation.4 | async-start | bytes 14598144 | tf_op jit(solution)/shard_map/reduce_scatter | solution.py:251
  542.6 11.7 %collective-permute-start.25 = (bf16[1,9,3456]{2,1,0:T(8,128)(2,1)S(1)}, bf16[1,9,3456]{2,1,0:T(8,128)(2,1)S(1)}, u32[]{:S(2)}, u32[]{:S(2)}) collective-permute-start(bf16[1,9,3456]{2,1,0:T(8,128)(2,1)S(1)} %get-tuple-element.57), channel_id=1, source_target_pairs={{0,1},{1,2},{2,3},{3,0},{4,5},{5,6},{6,7},{7,4},{8,9},{9,10},{10,1... | collective-permute-start | bytes 186632 | tf_op jit(solution)/shard_map/ppermute | solution.py:56
  544.9 18.3 %collective-permute-start.28 = (bf16[54,1152]{1,0:T(8,128)(2,1)S(1)}, bf16[54,1152]{1,0:T(8,128)(2,1)S(1)}, u32[]{:S(2)}, u32[]{:S(2)}) collective-permute-start(bf16[54,1152]{1,0:T(8,128)(2,1)S(1)} %pad_maximum_fusion.18), channel_id=1, source_target_pairs={{0,0},{4,1},{8,2},{12,3},{16,4},{20,5},{24,6},{28,7},{32,8},{36,9}... | collective-permute-start | bytes 373256 | tf_op jit(solution)/shard_map/ppermute | solution.py:264
  549.9 10.7 %collective-permute-start.27 = (bf16[1,9,3456]{2,1,0:T(8,128)(2,1)S(1)}, bf16[1,9,3456]{2,1,0:T(8,128)(2,1)S(1)}, u32[]{:S(2)}, u32[]{:S(2)}) collective-permute-start(bf16[1,9,3456]{2,1,0:T(8,128)(2,1)S(1)} %get-tuple-element.55), channel_id=1, source_target_pairs={{0,3},{1,0},{2,1},{3,2},{4,7},{5,4},{6,5},{7,6},{8,11},{9,8},{10,9... | collective-permute-start | bytes 186632 | tf_op jit(solution)/shard_map/ppermute | solution.py:56
  (90 other events, 949.1 us)
Sparse Core Ops, SparseCore 0:
  13.7 72.8 all-gather.4
  89.5 60.1 all-gather.6
  342.9 85.8 reduce-scatter.2
  433.0 108.3 reduce-scatter.4

commit v2 on v1

v2 whole, which is shorter than its diff:
```python
import math

import jax
import jax.numpy as jnp
from jax import lax
from jax.sharding import Mesh
from jax.sharding import PartitionSpec as P

norm_eps = 1e-06
rope_base = 1000000.0
score_scale = 0.0625
far_below = -1e30
f32 = jnp.float32
bf16 = jnp.bfloat16


def rms_norm(values, gain):
    factor = lax.rsqrt(jnp.mean(values * values, axis=-1, keepdims=True) + norm_eps)
    return values * factor * (1.0 + gain)


def rotate(values, cosine, sine):
    half_dim = values.shape[-1] // 2
    first_half = values[..., :half_dim]
    second_half = values[..., half_dim:]
    return jnp.concatenate(
        [first_half * cosine - second_half * sine, second_half * cosine + first_half * sine],
        axis=-1,
    )


def rope_tables(positions, head_dim):
    freq_index = jnp.arange(head_dim // 2, dtype=f32)
    inverse = jnp.exp(freq_index * (-2.0 / head_dim) * math.log(rope_base))
    angles = positions.astype(f32)[:, None] * inverse[None, :]
    return (jnp.cos(angles), jnp.sin(angles))


def gated_unit(gate_pre, up_pre):
    return jax.nn.gelu(gate_pre, approximate=True) * up_pre


def contract(left, right, left_dim, right_dim, kind=f32):
    return lax.dot_general(
        left, right, (((left_dim,), (right_dim,)), ((), ())), preferred_element_type=kind
    )


def from_ahead(block, step, axis="y"):
    size = lax.axis_size(axis)
    return lax.ppermute(block, axis, [(i, (i - step) % size) for i in range(size)])


def to_ahead(block, step, axis="y"):
    size = lax.axis_size(axis)
    return lax.ppermute(block, axis, [(i, (i + step) % size) for i in range(size)])


def gather_ahead(block, axis="y"):
    size = lax.axis_size(axis)
    return jnp.concatenate([block] + [from_ahead(block, s, axis) for s in range(1, size)], axis=0)


def sum_ahead(terms, axis="y"):
    arrived = [to_ahead(terms[s].astype(bf16), s, axis) for s in range(1, len(terms))]
    total = terms[0].astype(f32)
    for item in arrived:
        total = total + item.astype(f32)
    return total


def swap(pieces, axis):
    size = lax.axis_size(axis)
    me = lax.axis_index(axis)
    arrived = [lax.dynamic_index_in_dim(pieces, me, 0, keepdims=False)]
    for s in range(1, size):
        item = lax.dynamic_index_in_dim(pieces, (me + s) % size, 0, keepdims=False)
        arrived.append(to_ahead(item, s, axis))
    return by_sender(arrived, axis)


def by_sender(arrived, axis):
    size = lax.axis_size(axis)
    me = lax.axis_index(axis)
    result = []
    for c in range(size):
        item = arrived[0]
        for s in range(1, size):
            item = jnp.where((me - c) % size == s, arrived[s], item)
        result.append(item)
    return jnp.stack(result)


def gather_blocks(block, axis):
    size = lax.axis_size(axis)
    return by_sender([block] + [to_ahead(block, s, axis) for s in range(1, size)], axis)


def gather_team(block):
    return gather_ahead(gather_ahead(block, "y"), "core")


def sum_team(term, tokens):
    half = term.shape[0] // 2
    term = sum_ahead([term[:half], term[half:]], "core")
    return sum_ahead([term[i : i + tokens] for i in range(0, half, tokens)], "y")


def down_routes(teams, members):
    here, before = [], []
    for member in range(members):
        for block in range(teams):
            owner = member * teams + block
            here.append((owner, block * members + member))
            if block > 0:
                before.append((owner, (block - 1) * members + member))
    return here, before


def local(
    activations,
    cotangent,
    segments,
    in_gain,
    query_gain,
    key_gain,
    post_attn_gain,
    pre_ff_gain,
    post_ff_gain,
    w_query,
    w_key,
    w_value,
    w_out,
    w_gate,
    w_up,
    w_down,
):
    all_axes = ("x", "z", "core", "y")
    teams = lax.axis_size("x") * lax.axis_size("z")
    inner = lax.axis_size("y")
    cores = lax.axis_size("core")
    members = inner * cores
    me = lax.axis_index("y")
    team = lax.axis_index("x") * lax.axis_size("z") + lax.axis_index("z")
    flat = team * members + lax.axis_index("core") * inner + me
    rows = w_query.shape[0]
    model = w_down.shape[1]
    query_cols = w_query.shape[1]
    head_dim = w_key.shape[1]
    heads = query_cols // head_dim
    qkv_cols = query_cols + 2 * head_dim
    out_rows = w_out.shape[0]
    team_rows = members * rows
    part = w_gate.shape[1] // members
    wide = -(-part // 128) * 128
    down_rows = w_down.shape[0]
    down_wide = wide // teams
    down_shift = down_wide - down_rows

    def columns(weight):
        pieces = weight.reshape(rows, members, part)
        return jnp.pad(pieces, ((0, 0), (0, 0), (0, wide - part)))

    both = jnp.concatenate([columns(w_gate), columns(w_up)], axis=2).transpose(1, 0, 2)
    both = both.reshape(cores, inner, rows, 2 * wide)
    gains = (in_gain, query_gain, key_gain, post_attn_gain, pre_ff_gain, post_ff_gain)
    gain_row = jnp.concatenate(gains)
    gain_row = jnp.pad(gain_row, (0, model - gain_row.shape[0]))[None]
    attn_rows = jnp.concatenate(
        [w_query, w_key, w_value, jnp.concatenate([w_out, gain_row], axis=0)], axis=1
    )
    first_message = jnp.concatenate(
        [
            both.transpose(1, 2, 0, 3).reshape(inner, rows, cores * 2 * wide),
            jnp.broadcast_to(attn_rows[None], (inner,) + attn_rows.shape),
        ],
        axis=2,
    )
    by_y = swap(first_message, "y")
    attn_y = by_y[:, :, cores * 2 * wide :]
    second_message = jnp.stack(
        [
            jnp.concatenate([by_y[:, :, c * 2 * wide : (c + 1) * 2 * wide], attn_y], axis=2)
            for c in range(cores)
        ]
    )
    by_member = swap(second_message, "core").reshape(members, rows, -1)
    out_part = by_member[:, :, 2 * wide + qkv_cols :]
    here, before = down_routes(teams, members)
    down_two = jnp.concatenate(
        [lax.ppermute(w_down, all_axes, here), lax.ppermute(w_down, all_axes, before)], axis=0
    )
    down_part = lax.dynamic_slice_in_dim(down_two, down_shift * team, down_wide, 0)
    shard = jnp.concatenate(
        [
            by_member[:, :, : 2 * wide].reshape(team_rows, 2 * wide),
            jnp.pad(down_part, ((0, team_rows - down_wide), (0, 0))),
            by_member[:, :, 2 * wide : 2 * wide + qkv_cols].reshape(team_rows, qkv_cols),
            jnp.concatenate(
                [out_part[:, :out_rows].reshape(members * out_rows, model), out_part[:, out_rows]],
                axis=0,
            ),
        ],
        axis=1,
    )
    full = lax.all_gather(shard, ("x", "z"), axis=0, tiled=True)
    first = 2 * wide
    full_both = full[:, :first]
    by_team = full.reshape(teams, team_rows, -1)
    full_down = by_team[:, :down_wide, first : first + model].reshape(wide, model)
    first += model
    full_qkv = full[:, first : first + qkv_cols]
    first += qkv_cols
    full_out = by_team[:, : members * out_rows, first : first + model].reshape(query_cols, model)
    gain_all = by_team[:, members * out_rows :, first : first + 128].astype(f32)
    full_gains = []
    first = 0
    for item in gains:
        size = item.shape[0]
        full_gains.append(gain_all[:, :, first : first + size].reshape(-1))
        first += size
    gain_in, gain_query, gain_key, gain_post_attn, gain_pre, gain_post = full_gains

    inputs = activations[0].astype(f32)
    segment_all = segments[0]
    tok_count = inputs.shape[0]
    first_place = me * tok_count
    place_rows = first_place + jnp.arange(tok_count, dtype=jnp.int32)
    segment_rows = lax.dynamic_slice_in_dim(segment_all, first_place, tok_count)
    earlier = jnp.sum((segment_all[None, :] < segment_rows[:, None]).astype(jnp.int32), axis=1)
    cosine, sine = rope_tables(place_rows - earlier, head_dim)
    length = segment_all.shape[0]
    key_places = (first_place + jnp.arange(length, dtype=jnp.int32)) % length
    key_segments = jnp.take(segment_all, key_places)
    allowed = (segment_rows[:, None] == key_segments[None, :]) & (
        place_rows[:, None] >= key_places[None, :]
    )
    allowed = jnp.tile(allowed, (heads, 1))

    normed, in_pull = jax.vjp(rms_norm, inputs, gain_in)
    normed_low = normed.astype(bf16)
    qkv = contract(normed_low, full_qkv, 1, 0)
    query_raw = qkv[:, :query_cols].reshape(tok_count, heads, head_dim)
    key_raw = qkv[:, query_cols : query_cols + head_dim]
    value_low = qkv[:, query_cols + head_dim :].astype(bf16)

    def prepare(query_in, key_in, query_scale, key_scale):
        rotated_query = rotate(
            rms_norm(query_in, query_scale), cosine[:, None, :], sine[:, None, :]
        )
        rotated_key = rotate(rms_norm(key_in, key_scale), cosine, sine)
        return (rotated_query, rotated_key)

    (queries, key_rows), prepare_pull = jax.vjp(prepare, query_raw, key_raw, gain_query, gain_key)
    query_low = queries.astype(bf16).transpose(1, 0, 2).reshape(heads * tok_count, head_dim)
    key_value = gather_ahead(jnp.concatenate([key_rows.astype(bf16), value_low], axis=1))
    key_all = key_value[:, :head_dim]
    value_all = key_value[:, head_dim:]

    scores = contract(query_low, key_all, 1, 1) * score_scale
    scores = jnp.where(allowed, scores, far_below)
    top_score = jnp.max(scores, axis=-1, keepdims=True)
    weight = jnp.exp(scores - top_score)
    prob = weight / jnp.sum(weight, axis=-1, keepdims=True)
    prob_low = prob.astype(bf16)
    attended = contract(prob_low, value_all, 1, 0).astype(bf16)
    attended_low = attended.reshape(heads, tok_count, head_dim).transpose(1, 0, 2)
    attended_low = attended_low.reshape(tok_count, query_cols)
    attn_out = contract(attended_low, full_out, 1, 0)
    post_attn, post_attn_pull = jax.vjp(rms_norm, attn_out, gain_post_attn)
    middle = inputs + post_attn
    normed_ff, pre_pull = jax.vjp(rms_norm, middle, gain_pre)
    normed_all = gather_team(normed_ff.astype(bf16))

    gate_up = contract(normed_all, full_both, 1, 0)
    mixed, gated_pull = jax.vjp(gated_unit, gate_up[:, :wide], gate_up[:, wide:])
    mixed_low = mixed.astype(bf16)
    branch_term = contract(mixed_low, full_down, 1, 0)
    branch_out = sum_team(branch_term, tok_count)
    post_ff, post_pull = jax.vjp(rms_norm, branch_out, gain_post)
    output = (middle + post_ff).astype(bf16)

    grad_output = cotangent[0].astype(f32)
    grad_branch, grad_post_ff = post_pull(grad_output)
    grad_branch_all = gather_team(grad_branch.astype(bf16))
    down_term = contract(mixed_low, grad_branch_all, 0, 0, bf16)
    grad_mixed = contract(grad_branch_all, full_down, 1, 1)
    grad_gate, grad_up = gated_pull(grad_mixed)
    grad_both = jnp.concatenate([grad_gate.astype(bf16), grad_up.astype(bf16)], axis=1)
    both_term = contract(normed_all, grad_both, 0, 0, bf16)
    grad_normed_term = contract(grad_both, full_both, 1, 1)
    ffn_terms = jnp.concatenate(
        [
            both_term.reshape(teams, team_rows, 2 * wide),
            jnp.pad(
                down_term.reshape(teams, down_wide, model),
                ((0, 0), (0, team_rows - down_wide), (0, 0)),
            ),
        ],
        axis=2,
    ).reshape(teams * team_rows, -1)
    ffn_terms, grad_normed_term = lax.optimization_barrier((ffn_terms, grad_normed_term))
    ffn_sum = lax.psum_scatter(ffn_terms.reshape(teams, team_rows, -1), ("x", "z"), scatter_dimension=0, tiled=True)[0]
    both_grad = ffn_sum[:, : 2 * wide].reshape(cores, inner, rows, 2 * wide).transpose(1, 0, 2, 3)
    both_grad = swap(both_grad, "y").transpose(1, 0, 2, 3)
    both_grad = swap(both_grad, "core").reshape(members, rows, 2 * wide).astype(f32)
    both_grad = both_grad.transpose(1, 0, 2)
    gate_grad = both_grad[:, :, :part].reshape(rows, members * part)
    up_grad = both_grad[:, :, wide : wide + part].reshape(rows, members * part)
    down_sum = ffn_sum[:down_wide, 2 * wide :]
    down_two = jnp.concatenate(
        [
            lax.ppermute(down_sum, all_axes, [(b, a) for a, b in before]),
            lax.ppermute(down_sum, all_axes, [(b, a) for a, b in here]),
        ],
        axis=0,
    )
    down_grad = lax.dynamic_slice_in_dim(
        down_two, down_wide - down_shift * (flat % teams), down_rows, 0
    ).astype(f32)

    grad_normed_ff = sum_team(grad_normed_term, tok_count)
    grad_middle_add, grad_pre_ff = pre_pull(grad_normed_ff)
    grad_middle = grad_output + grad_middle_add
    grad_attn, grad_post_attn = post_attn_pull(grad_middle)
    grad_attn_low = grad_attn.astype(bf16)
    out_term = contract(attended_low, grad_attn_low, 0, 0, bf16)
    grad_attended = contract(grad_attn_low, full_out, 1, 1, bf16)
    grad_attended = grad_attended.reshape(tok_count, heads, head_dim).transpose(1, 0, 2)
    grad_attended = grad_attended.reshape(heads * tok_count, head_dim)

    grad_prob = contract(grad_attended, value_all, 1, 1)
    shift_term = jnp.sum(prob * grad_prob, axis=-1, keepdims=True)
    grad_scores = (prob * (grad_prob - shift_term)).astype(bf16)
    grad_query = contract(grad_scores, key_all, 1, 0) * score_scale
    grad_key = contract(grad_scores, query_low, 0, 0) * score_scale
    grad_value = contract(prob_low, grad_attended, 0, 0)
    grad_key_value = jnp.concatenate([grad_key, grad_value], axis=1)
    grad_key_value = sum_ahead(
        [grad_key_value[s * tok_count : (s + 1) * tok_count] for s in range(inner)]
    )
    grad_queries = grad_query.reshape(heads, tok_count, head_dim).transpose(1, 0, 2)
    grad_query_raw, grad_key_raw, grad_query_gain, grad_key_gain = prepare_pull(
        (grad_queries, grad_key_value[:, :head_dim])
    )
    grad_qkv = jnp.concatenate(
        [
            grad_query_raw.reshape(tok_count, query_cols),
            grad_key_raw,
            grad_key_value[:, head_dim:],
        ],
        axis=1,
    ).astype(bf16)
    qkv_term = contract(normed_low, grad_qkv, 0, 0, bf16)
    grad_normed = contract(grad_qkv, full_qkv, 1, 1)
    grad_input_add, grad_in_gain = in_pull(grad_normed)
    input_grad = grad_middle + grad_input_add

    grad_gains = (
        grad_in_gain,
        grad_query_gain,
        grad_key_gain,
        grad_post_attn,
        grad_pre_ff,
        grad_post_ff,
    )
    gain_terms = jnp.concatenate(
        [item.reshape(teams, members, -1) for item in grad_gains], axis=2
    ).astype(bf16)
    filling = jnp.broadcast_to(ffn_sum[0, 0], gain_terms.shape[:2] + (model - gain_terms.shape[2],))
    gain_terms = jnp.concatenate([gain_terms, filling], axis=2)
    attn_terms = jnp.concatenate(
        [
            qkv_term.reshape(teams, team_rows, qkv_cols),
            jnp.concatenate(
                [out_term.reshape(teams, members * out_rows, model), gain_terms], axis=1
            ),
        ],
        axis=2,
    ).reshape(teams * team_rows, -1)
    attn_sum = lax.psum_scatter(attn_terms.reshape(teams, team_rows, -1), ("x", "z"), scatter_dimension=0, tiled=True)[0]
    attn_sum = jnp.concatenate(
        [
            attn_sum[:, :qkv_cols].reshape(members, rows, qkv_cols),
            jnp.concatenate(
                [
                    attn_sum[: members * out_rows, qkv_cols:].reshape(members, out_rows, model),
                    attn_sum[members * out_rows :, qkv_cols:][:, None],
                ],
                axis=1,
            ),
        ],
        axis=2,
    ).reshape(cores, inner, rows, qkv_cols + model)
    attn_sum = jnp.sum(swap(attn_sum.transpose(1, 0, 2, 3), "y").astype(f32), axis=0)
    attn_grad = jnp.sum(swap(attn_sum.astype(bf16), "core").astype(f32), axis=0)
    gain_grads = []
    first = qkv_cols
    for item in gains:
        size = item.shape[0]
        gain_grads.append(attn_grad[rows - 1, first : first + size])
        first += size
    return (
        output[None],
        input_grad[None],
        *gain_grads,
        attn_grad[:, :query_cols],
        attn_grad[:, query_cols : query_cols + head_dim],
        attn_grad[:, query_cols + head_dim : qkv_cols],
        attn_grad[:out_rows, qkv_cols:],
        gate_grad,
        up_grad,
        down_grad,
    )


def solution(mesh):
    fine = Mesh(mesh.devices.reshape(4, 4, 2, 4), ("x", "z", "core", "y"))
    all_axes = ("x", "z", "core", "y")
    shard = P(all_axes)
    matrix = P(all_axes, None)
    tokens = P(("x", "z", "core"), "y", None)
    return jax.shard_map(
        local,
        mesh=fine,
        in_specs=(tokens, tokens, P(("x", "z", "core"), None)) + (shard,) * 6 + (matrix,) * 7,
        out_specs=(tokens, tokens) + (shard,) * 6 + (matrix,) * 7,
        check_vma=False,
    )
```

time: 582 us -> 503 us (0.86)
  local copies, waits for them, and re-layouts: 150 us -> 49.3 us
  starting transfers between devices: 50.3 us -> 76 us
  waiting for transfers between devices: 234 us -> 253 us
  matrix products: 67.2 us -> 51.2 us
    reduce_scatter x2 -> x0, waiting for transfers between devices: 117 us -> none  [the longest x1 101 us: local(): lax.psum_scatter(ffn_terms.reshape(-1, 2 * part), 'dp', scatter_dimension...]
    unnamed x4 -> x5, waiting for transfers between devices: 0.07 us -> 88.5 us
    reshape x28 -> x16, local copies, waits for them, and re-layouts: 78.4 us -> 8.75 us  [the longest x6 3.93 us: local(): item.reshape(teams, members, -1)]
    ppermute x29 -> x38, starting transfers between devices: 49.6 us -> 75.9 us  [the longest x23 29.7 us: to_ahead(): lax.ppermute(block, axis, [(i, (i + step) % size) for i in range(size)])]
    all_gather x2 -> x1, waiting for transfers between devices: 70.5 us -> 95.2 us  [local(): full = lax.all_gather(shard, ('x', 'z'), axis=0, tiled=True)]
    ppermute x29 -> x38, waiting for transfers between devices: 47 us -> 68.9 us  [the longest x23 35.1 us: to_ahead(): lax.ppermute(block, axis, [(i, (i + step) % size) for i in range(size)])]
    dot_general x19 -> x18, matrix products: 67.2 us -> 51.2 us  [contract(): lax.dot_general(left, right, (((left_dim,), (right_dim,)), ((), ())), pre...]
    concatenate x6 -> x10, other arithmetic: 27.4 us -> 17.2 us  [the longest x1 7.3 us: local(): jnp.concatenate([qkv_term.reshape(teams, team_rows, qkv_cols), jnp.concat...]
  transfers between devices with their start and end apart: 33 -> 41, of which waited for: 15 -> 24; matrix products, arithmetic and copies ran while one was open for 31% -> 10% of each run, Pallas kernels for 0% -> 0%
where the time goes in v2:
time: 503 us; the launch traced here: 494 us
  waiting for transfers between devices  253 us (50%)
  starting transfers between devices  76 us (15%)
  matrix products  51.2 us (10%)
  local copies, waits for them, and re-layouts  49.3 us (10%)
  other arithmetic  48.7 us (10%)
  between operations  16.1 us (3%)
    all_gather x1, waiting for transfers between devices, local(): full = lax.all_gather(shard, ('x', 'z'), axis=0, tiled=True)  95.2 us
    unnamed x5, waiting for transfers between devices  88.5 us
    dot_general x18, matrix products, contract(): lax.dot_general(left, right, (((left_dim,), (right_dim,)), ((), ())), pre...  51.2 us
    ppermute x23, waiting for transfers between devices, to_ahead(): lax.ppermute(block, axis, [(i, (i + step) % size) for i in range(size)])  35.1 us
    ppermute x23, starting transfers between devices, to_ahead(): lax.ppermute(block, axis, [(i, (i + step) % size) for i in range(size)])  29.7 us
    ppermute x11, waiting for transfers between devices, from_ahead(): lax.ppermute(block, axis, [(i, (i - step) % size) for i in range(size)])  28.3 us
    ppermute x11, starting transfers between devices, from_ahead(): lax.ppermute(block, axis, [(i, (i - step) % size) for i in range(size)])  24.7 us
  transfers between devices with their start and end apart: 41, of which 24 were waited for; matrix products, arithmetic and copies ran while one was open for 10% of the time, Pallas kernels for 0%

profile of v2, /device:TPU:1, one launch (start us, length us, event | category | flops | bytes accessed | tf_op | source)
XLA Modules:
  0.0 493.9 jit_solution(5527310317802538896)
XLA Ops:
  7.3 4.1 concatenate.104
  22.1 7.1 %collective-permute-start.5 = (bf16[54,1152]{1,0:T(8,128)(2,1)S(1)}, bf16[54,1152]{1,0:T(8,128)(2,1)S(1)}, u32[]{:S(2)}, u32[]{:S(2)}) collective-permute-start(bf16[54,1152]{1,0:T(8,128)(2,1)S(1)} %copy-done.67), channel_id=1, source_target_pairs={{1,0},{2,8},{3,16},{4,24},{5,32},{6,40},{7,48},{8,56},{9,64},{10,7... | collective-permute-start | bytes 373256 | tf_op jit(solution)/shard_map/ppermute | solution.py:191
  33.0 4.0 collective-permute-done.4
  45.2 95.2 %all-gather.2.cloned.1.call-done = bf16[1152,5632]{1,0:T(8,128)(2,1)} async-done(((bf16[72,5632]{1,0:T(8,128)(2,1)}), bf16[1152,5632]{1,0:T(8,128)(2,1)}) %all-gather.2.cloned.1.call-update) | async-done | bytes 12976144 | tf_op jit(solution)/shard_map/all_gather | solution.py:206
  168.7 3.8 collective-permute-done.11
  172.6 7.1 %collective-permute-done.10 = bf16[128,1152]{1,0:T(8,128)(2,1)S(1)} collective-permute-done((bf16[128,1152]{1,0:T(8,128)(2,1)S(1)}, bf16[128,1152]{1,0:T(8,128)(2,1)S(1)}, u32[]{:S(2)}, u32[]{:S(2)}) %collective-permute-start.10) | collective-permute-done | bytes 294944 | tf_op jit(solution)/shard_map/ppermute | solution.py:51
  186.3 7.1 %fusion.14 = f32[1024,1792]{1,0:T(8,128)S(1)} fusion(bf16[1024,1152]{1,0:T(8,128)(2,1)S(1)} %constant_dynamic-update-slice_fusion, bf16[1152,5632]{1,0:T(8,128)(2,1)} %all-gather.2.cloned.1.call-done), kind=kOutput, calls=%fused_computation.23 | convolution fusion | flops 4227858432 | bytes 13828096 | tf_op jit(solution)/shard_map/dot_general | solution.py:44
  210.2 4.4 collective-permute-done.14
  214.6 7.1 %collective-permute-done.15 = bf16[128,1152]{1,0:T(8,128)(2,1)} collective-permute-done((bf16[128,1152]{1,0:T(8,128)(2,1)}, bf16[128,1152]{1,0:T(8,128)(2,1)}, u32[]{:S(2)}, u32[]{:S(2)}) %collective-permute-start.15) | collective-permute-done | bytes 294944 | tf_op jit(solution)/shard_map/ppermute | solution.py:56
  229.1 5.9 %collective-permute-done.19 = bf16[128,1152]{1,0:T(8,128)(2,1)S(1)} collective-permute-done((bf16[128,1152]{1,0:T(8,128)(2,1)S(1)}, bf16[128,1152]{1,0:T(8,128)(2,1)S(1)}, u32[]{:S(2)}, u32[]{:S(2)}) %collective-permute-start.19) | collective-permute-done | bytes 294944 | tf_op jit(solution)/shard_map/ppermute | solution.py:51
  235.0 5.5 %collective-permute-done.18 = bf16[128,1152]{1,0:T(8,128)(2,1)S(1)} collective-permute-done((bf16[128,1152]{1,0:T(8,128)(2,1)S(1)}, bf16[128,1152]{1,0:T(8,128)(2,1)S(1)}, u32[]{:S(2)}, u32[]{:S(2)}) %collective-permute-start.18) | collective-permute-done | bytes 294944 | tf_op jit(solution)/shard_map/ppermute | solution.py:51
  242.2 10.4 %collective-permute-start.20 = (bf16[512,1152]{1,0:T(8,128)(2,1)S(1)}, bf16[512,1152]{1,0:T(8,128)(2,1)S(1)}, u32[]{:S(2)}, u32[]{:S(2)}) collective-permute-start(bf16[512,1152]{1,0:T(8,128)(2,1)S(1)} %pad_maximum_fusion.6), channel_id=1, source_target_pairs={{0,4},{4,0},{1,5},{5,1},{2,6},{6,2},{3,7},{7,3},{8,12},{12,8},{9,1... | collective-permute-start | bytes 3538952 | tf_op jit(solution)/shard_map/ppermute | solution.py:51
  255.3 7.1 %fusion.11 = (bf16[1024,896]{1,0:T(8,128)(2,1)S(1)}, bf16[1024,896]{1,0:T(8,128)(2,1)S(1)}) fusion(f32[1024,1792]{1,0:T(8,128)} %copy-done.3, bf16[1024,1152]{1,0:T(8,128)(2,1)S(1)} %constant_dynamic-update-slice_fusion.5, bf16[896,1152]{1,0:T(8,128)(2,1)S(1)} %bitcast.303), kind=kOutput, calls=%fused_computation.17 | convolution fusion | flops 2135949312 | bytes 15433728 | tf_op jit(solution)/shard_map/dot_general | solution.py:44
  266.8 6.9 %fusion.20 = bf16[1152,1792]{1,0:T(8,128)(2,1)} fusion(bf16[1024,1152]{1,0:T(8,128)(2,1)S(1)} %copy-done.33, bf16[1024,896]{1,0:T(8,128)(2,1)S(1)} %get-tuple-element.48, bf16[1024,896]{1,0:T(8,128)(2,1)S(1)} %get-tuple-element.47), kind=kOutput, calls=%fused_computation.32 | convolution fusion | flops 4235198464 | bytes 10158080 | tf_op jit(solution)/shard_map/dot_general | solution.py:44
  273.7 5.5 %pad_maximum_fusion = bf16[1152,2944]{1,0:T(8,128)(2,1)} fusion(bf16[1152,1152]{1,0:T(8,128)(2,1)S(1)} %bitcast.298, bf16[1152,1792]{1,0:T(8,128)(2,1)} %fusion.20), kind=kLoop, calls=%fused_computation.6 | loop fusion | flops 13565952 | bytes 13565952 | tf_op jit(solution)/shard_map/concatenate | solution.py:292
  279.2 9.9 %fusion.12 = f32[1024,1152]{1,0:T(8,128)} fusion(bf16[1152,5632]{1,0:T(8,128)(2,1)} %all-gather.2.cloned.1.call-done, bf16[1024,896]{1,0:T(8,128)(2,1)} %copy-done.70, bf16[1024,896]{1,0:T(8,128)(2,1)S(1)} %copy-done.69), kind=kOutput, calls=%fused_computation.21 | convolution fusion | flops 4235198464 | bytes 12517376 | tf_op jit(solution)/shard_map/dot_general | solution.py:44
  303.5 4.7 collective-permute-done.22
  308.2 7.2 %collective-permute-done.23 = bf16[128,1152]{1,0:T(8,128)(2,1)} collective-permute-done((bf16[128,1152]{1,0:T(8,128)(2,1)}, bf16[128,1152]{1,0:T(8,128)(2,1)}, u32[]{:S(2)}, u32[]{:S(2)}) %collective-permute-start.23) | collective-permute-done | bytes 294944 | tf_op jit(solution)/shard_map/ppermute | solution.py:56
  347.5 24.3 %reduce-scatter.7.cloned.1.call-done = bf16[1,72,2944]{2,1,0:T(8,128)(2,1)} async-done(((bf16[16,72,2944]{2,1,0:T(8,128)(2,1)}), bf16[1,72,2944]{2,1,0:T(8,128)(2,1)}) %reduce-scatter.7.cloned.1.call-update) | async-done | bytes 423952
  373.0 7.3 %fusion.4 = bf16[16,72,2688]{2,1,0:T(8,128)(2,1)} fusion(bf16[16,8,40]{2,1,0:T(8,128)(2,1)} %concatenate.125, bf16[]{:T(256)} %bitcast.51, bf16[16,64,1152]{2,1,0:T(8,128)(2,1)} %fusion.177, bf16[16,72,1536]{2,1,0:T(8,128)(2,1)S(1)} %fusion.72), kind=kLoop, calls=%fused_computation.8 | loop fusion | flops 34062336 | bytes 12101634 | tf_op jit(solution)/shard_map/concatenate | solution.py:372
  385.3 6.7 %collective-permute-start.37 = (bf16[56,1152]{1,0:T(8,128)(2,1)S(1)}, bf16[56,1152]{1,0:T(8,128)(2,1)S(1)}, u32[]{:S(2)}, u32[]{:S(2)}) collective-permute-start(bf16[56,1152]{1,0:T(8,128)(2,1)S(1)} %slice.335), channel_id=1, source_target_pairs={{0,0},{8,1},{16,2},{24,3},{32,4},{40,5},{48,6},{56,7},{64,8},{72,9... | collective-permute-start | bytes 387080 | tf_op jit(solution)/shard_map/ppermute | solution.py:314
  391.9 5.8 %collective-permute-start.36 = (bf16[56,1152]{1,0:T(8,128)(2,1)S(1)}, bf16[56,1152]{1,0:T(8,128)(2,1)S(1)}, u32[]{:S(2)}, u32[]{:S(2)}) collective-permute-start(bf16[56,1152]{1,0:T(8,128)(2,1)S(1)} %slice.335), channel_id=1, source_target_pairs={{0,1},{8,2},{16,3},{24,4},{32,5},{40,6},{48,7},{56,8},{64,9},{72,1... | collective-permute-start | bytes 387080 | tf_op jit(solution)/shard_map/ppermute | solution.py:313
  401.9 64.1 %reduce-scatter.9.cloned.1.call-done = bf16[1,72,2688]{2,1,0:T(8,128)(2,1)} async-done(((bf16[16,72,2688]{2,1,0:T(8,128)(2,1)}), bf16[1,72,2688]{2,1,0:T(8,128)(2,1)}) %reduce-scatter.9.cloned.1.call-update) | async-done | bytes 387088
  474.5 4.1 collective-permute-done.29
  (389 shorter events, 162.6 us)
Async XLA Ops:
  7.2 133.2 %all-gather.2.cloned.1.call-start = ((), (), s32[]{:S(2)}) async-start(), calls=%async_computation.2 | async-start | bytes 13787136 | tf_op jit(solution)/shard_map/all_gather | solution.py:206
  16.0 15.2 %collective-permute-start.2 = (bf16[9,6272]{1,0:T(8,128)(2,1)S(1)}, bf16[9,6272]{1,0:T(8,128)(2,1)S(1)}, u32[]{:S(2)}, u32[]{:S(2)}) collective-permute-start(bf16[9,6272]{1,0:T(8,128)(2,1)S(1)} %bitcast.328), channel_id=1, source_target_pairs={{0,1},{1,2},{2,3},{3,0},{4,5},{5,6},{6,7},{7,4},{8,9},{9,10},{10,1... | collective-permute-start | bytes 338696 | tf_op jit(solution)/shard_map/ppermute | solution.py:56
  18.3 13.0 %collective-permute-start.1 = (bf16[9,6272]{1,0:T(8,128)(2,1)S(1)}, bf16[9,6272]{1,0:T(8,128)(2,1)S(1)}, u32[]{:S(2)}, u32[]{:S(2)}) collective-permute-start(bf16[9,6272]{1,0:T(8,128)(2,1)S(1)} %bitcast.329), channel_id=1, source_target_pairs={{0,2},{1,3},{2,0},{3,1},{4,6},{5,7},{6,4},{7,5},{8,10},{9,11},{10,... | collective-permute-start | bytes 338696 | tf_op jit(solution)/shard_map/ppermute | solution.py:56
  21.0 10.3 %collective-permute-start = (bf16[9,6272]{1,0:T(8,128)(2,1)S(1)}, bf16[9,6272]{1,0:T(8,128)(2,1)S(1)}, u32[]{:S(2)}, u32[]{:S(2)}) collective-permute-start(bf16[9,6272]{1,0:T(8,128)(2,1)S(1)} %bitcast.330), channel_id=1, source_target_pairs={{0,3},{1,0},{2,1},{3,2},{4,7},{5,4},{6,5},{7,6},{8,11},{9,8},{10,9... | collective-permute-start | bytes 338696 | tf_op jit(solution)/shard_map/ppermute | solution.py:56
  22.1 10.9 %collective-permute-start.5 = (bf16[54,1152]{1,0:T(8,128)(2,1)S(1)}, bf16[54,1152]{1,0:T(8,128)(2,1)S(1)}, u32[]{:S(2)}, u32[]{:S(2)}) collective-permute-start(bf16[54,1152]{1,0:T(8,128)(2,1)S(1)} %copy-done.67), channel_id=1, source_target_pairs={{1,0},{2,8},{3,16},{4,24},{5,32},{6,40},{7,48},{8,56},{9,64},{10,7... | collective-permute-start | bytes 373256 | tf_op jit(solution)/shard_map/ppermute | solution.py:191
  39.8 331.9 %reduce-scatter.7.cloned.1.call-start = ((), (), s32[]{:S(2)}) async-start(), calls=%async_computation.3 | async-start | bytes 7206912
  146.9 8.9 %collective-permute-start.8 = (bf16[128,512]{1,0:T(8,128)(2,1)S(1)}, bf16[128,512]{1,0:T(8,128)(2,1)}, u32[]{:S(2)}, u32[]{:S(2)}) collective-permute-start(bf16[128,512]{1,0:T(8,128)(2,1)S(1)} %pad_maximum_fusion.17), channel_id=1, source_target_pairs={{0,1},{1,2},{2,3},{3,0},{4,5},{5,6},{6,7},{7,4},{8,9},{9,10},{10,1... | collective-permute-start | bytes 393224 | tf_op jit(solution)/shard_map/ppermute | solution.py:51
  166.3 13.4 %collective-permute-start.10 = (bf16[128,1152]{1,0:T(8,128)(2,1)S(1)}, bf16[128,1152]{1,0:T(8,128)(2,1)S(1)}, u32[]{:S(2)}, u32[]{:S(2)}) collective-permute-start(bf16[128,1152]{1,0:T(8,128)(2,1)S(1)} %get-tuple-element.44), channel_id=1, source_target_pairs={{0,2},{1,3},{2,0},{3,1},{4,6},{5,7},{6,4},{7,5},{8,10},{9,11},{10,... | collective-permute-start | bytes 884744 | tf_op jit(solution)/shard_map/ppermute | solution.py:51
  167.7 12.7 %collective-permute-start.9 = (bf16[128,1152]{1,0:T(8,128)(2,1)S(1)}, bf16[128,1152]{1,0:T(8,128)(2,1)S(1)}, u32[]{:S(2)}, u32[]{:S(2)}) collective-permute-start(bf16[128,1152]{1,0:T(8,128)(2,1)S(1)} %get-tuple-element.44), channel_id=1, source_target_pairs={{0,3},{1,0},{2,1},{3,2},{4,7},{5,4},{6,5},{7,6},{8,11},{9,8},{10,9... | collective-permute-start | bytes 884744 | tf_op jit(solution)/shard_map/ppermute | solution.py:51
  204.9 9.7 %collective-permute-start.14 = (bf16[128,1152]{1,0:T(8,128)(2,1)}, bf16[128,1152]{1,0:T(8,128)(2,1)}, u32[]{:S(2)}, u32[]{:S(2)}) collective-permute-start(bf16[128,1152]{1,0:T(8,128)(2,1)} %get-tuple-element.52), channel_id=1, source_target_pairs={{0,1},{1,2},{2,3},{3,0},{4,5},{5,6},{6,7},{7,4},{8,9},{9,10},{10,1... | collective-permute-start | bytes 884744 | tf_op jit(solution)/shard_map/ppermute | solution.py:56
  207.5 14.2 %collective-permute-start.15 = (bf16[128,1152]{1,0:T(8,128)(2,1)}, bf16[128,1152]{1,0:T(8,128)(2,1)}, u32[]{:S(2)}, u32[]{:S(2)}) collective-permute-start(bf16[128,1152]{1,0:T(8,128)(2,1)} %get-tuple-element.54), channel_id=1, source_target_pairs={{0,2},{1,3},{2,0},{3,1},{4,6},{5,7},{6,4},{7,5},{8,10},{9,11},{10,... | collective-permute-start | bytes 884744 | tf_op jit(solution)/shard_map/ppermute | solution.py:56
  226.0 9.0 %collective-permute-start.19 = (bf16[128,1152]{1,0:T(8,128)(2,1)S(1)}, bf16[128,1152]{1,0:T(8,128)(2,1)S(1)}, u32[]{:S(2)}, u32[]{:S(2)}) collective-permute-start(bf16[128,1152]{1,0:T(8,128)(2,1)S(1)} %get-tuple-element.38), channel_id=1, source_target_pairs={{0,1},{1,2},{2,3},{3,0},{4,5},{5,6},{6,7},{7,4},{8,9},{9,10},{10,1... | collective-permute-start | bytes 884744 | tf_op jit(solution)/shard_map/ppermute | solution.py:51
  226.6 13.9 %collective-permute-start.18 = (bf16[128,1152]{1,0:T(8,128)(2,1)S(1)}, bf16[128,1152]{1,0:T(8,128)(2,1)S(1)}, u32[]{:S(2)}, u32[]{:S(2)}) collective-permute-start(bf16[128,1152]{1,0:T(8,128)(2,1)S(1)} %get-tuple-element.38), channel_id=1, source_target_pairs={{0,2},{1,3},{2,0},{3,1},{4,6},{5,7},{6,4},{7,5},{8,10},{9,11},{10,... | collective-permute-start | bytes 884744 | tf_op jit(solution)/shard_map/ppermute | solution.py:51
  228.8 13.4 %collective-permute-start.17 = (bf16[128,1152]{1,0:T(8,128)(2,1)S(1)}, bf16[128,1152]{1,0:T(8,128)(2,1)S(1)}, u32[]{:S(2)}, u32[]{:S(2)}) collective-permute-start(bf16[128,1152]{1,0:T(8,128)(2,1)S(1)} %get-tuple-element.38), channel_id=1, source_target_pairs={{0,3},{1,0},{2,1},{3,2},{4,7},{5,4},{6,5},{7,6},{8,11},{9,8},{10,9... | collective-permute-start | bytes 884744 | tf_op jit(solution)/shard_map/ppermute | solution.py:51
  242.2 12.9 %collective-permute-start.20 = (bf16[512,1152]{1,0:T(8,128)(2,1)S(1)}, bf16[512,1152]{1,0:T(8,128)(2,1)S(1)}, u32[]{:S(2)}, u32[]{:S(2)}) collective-permute-start(bf16[512,1152]{1,0:T(8,128)(2,1)S(1)} %pad_maximum_fusion.6), channel_id=1, source_target_pairs={{0,4},{4,0},{1,5},{5,1},{2,6},{6,2},{3,7},{7,3},{8,12},{12,8},{9,1... | collective-permute-start | bytes 3538952 | tf_op jit(solution)/shard_map/ppermute | solution.py:51
  289.1 177.0 %reduce-scatter.9.cloned.1.call-start = ((), (), s32[]{:S(2)}) async-start(), calls=%async_computation.4 | async-start | bytes 6580224
  298.2 9.9 %collective-permute-start.22 = (bf16[128,1152]{1,0:T(8,128)(2,1)}, bf16[128,1152]{1,0:T(8,128)(2,1)}, u32[]{:S(2)}, u32[]{:S(2)}) collective-permute-start(bf16[128,1152]{1,0:T(8,128)(2,1)} %get-tuple-element.49), channel_id=1, source_target_pairs={{0,1},{1,2},{2,3},{3,0},{4,5},{5,6},{6,7},{7,4},{8,9},{9,10},{10,1... | collective-permute-start | bytes 884744 | tf_op jit(solution)/shard_map/ppermute | solution.py:56
  298.7 9.4 %collective-permute-start.24 = (bf16[128,1152]{1,0:T(8,128)(2,1)}, bf16[128,1152]{1,0:T(8,128)(2,1)}, u32[]{:S(2)}, u32[]{:S(2)}) collective-permute-start(bf16[128,1152]{1,0:T(8,128)(2,1)} %get-tuple-element.50), channel_id=1, source_target_pairs={{0,3},{1,0},{2,1},{3,2},{4,7},{5,4},{6,5},{7,6},{8,11},{9,8},{10,9... | collective-permute-start | bytes 884744 | tf_op jit(solution)/shard_map/ppermute | solution.py:56
  301.1 14.2 %collective-permute-start.23 = (bf16[128,1152]{1,0:T(8,128)(2,1)}, bf16[128,1152]{1,0:T(8,128)(2,1)}, u32[]{:S(2)}, u32[]{:S(2)}) collective-permute-start(bf16[128,1152]{1,0:T(8,128)(2,1)} %get-tuple-element.51), channel_id=1, source_target_pairs={{0,2},{1,3},{2,0},{3,1},{4,6},{5,7},{6,4},{7,5},{8,10},{9,11},{10,... | collective-permute-start | bytes 884744 | tf_op jit(solution)/shard_map/ppermute | solution.py:56
  381.7 16.1 %collective-permute-start.32 = (bf16[2,9,1792]{2,0,1:T(2,128)(2,1)S(1)}, bf16[2,9,1792]{2,0,1:T(2,128)(2,1)S(1)}, u32[]{:S(2)}, u32[]{:S(2)}) collective-permute-start(bf16[2,9,1792]{2,0,1:T(2,128)(2,1)S(1)} %bitcast.334), channel_id=1, source_target_pairs={{0,3},{1,0},{2,1},{3,2},{4,7},{5,4},{6,5},{7,6},{8,11},{9,8},{10,9... | collective-permute-start | bytes 193544 | tf_op jit(solution)/shard_map/ppermute | solution.py:56
  384.1 13.6 %collective-permute-start.33 = (bf16[2,9,1792]{2,0,1:T(2,128)(2,1)S(1)}, bf16[2,9,1792]{2,0,1:T(2,128)(2,1)S(1)}, u32[]{:S(2)}, u32[]{:S(2)}) collective-permute-start(bf16[2,9,1792]{2,0,1:T(2,128)(2,1)S(1)} %bitcast.333), channel_id=1, source_target_pairs={{0,2},{1,3},{2,0},{3,1},{4,6},{5,7},{6,4},{7,5},{8,10},{9,11},{10,... | collective-permute-start | bytes 193544 | tf_op jit(solution)/shard_map/ppermute | solution.py:56
  384.7 13.1 %collective-permute-start.34 = (bf16[2,9,1792]{2,0,1:T(2,128)(2,1)S(1)}, bf16[2,9,1792]{2,0,1:T(2,128)(2,1)S(1)}, u32[]{:S(2)}, u32[]{:S(2)}) collective-permute-start(bf16[2,9,1792]{2,0,1:T(2,128)(2,1)S(1)} %bitcast.332), channel_id=1, source_target_pairs={{0,1},{1,2},{2,3},{3,0},{4,5},{5,6},{6,7},{7,4},{8,9},{9,10},{10,1... | collective-permute-start | bytes 193544 | tf_op jit(solution)/shard_map/ppermute | solution.py:56
  385.3 14.1 %collective-permute-start.37 = (bf16[56,1152]{1,0:T(8,128)(2,1)S(1)}, bf16[56,1152]{1,0:T(8,128)(2,1)S(1)}, u32[]{:S(2)}, u32[]{:S(2)}) collective-permute-start(bf16[56,1152]{1,0:T(8,128)(2,1)S(1)} %slice.335), channel_id=1, source_target_pairs={{0,0},{8,1},{16,2},{24,3},{32,4},{40,5},{48,6},{56,7},{64,8},{72,9... | collective-permute-start | bytes 387080 | tf_op jit(solution)/shard_map/ppermute | solution.py:314
  391.9 9.0 %collective-permute-start.36 = (bf16[56,1152]{1,0:T(8,128)(2,1)S(1)}, bf16[56,1152]{1,0:T(8,128)(2,1)S(1)}, u32[]{:S(2)}, u32[]{:S(2)}) collective-permute-start(bf16[56,1152]{1,0:T(8,128)(2,1)S(1)} %slice.335), channel_id=1, source_target_pairs={{0,1},{8,2},{16,3},{24,4},{32,5},{40,6},{48,7},{56,8},{64,9},{72,1... | collective-permute-start | bytes 387080 | tf_op jit(solution)/shard_map/ppermute | solution.py:313
  (88 other events, 775.9 us)
Sparse Core Ops, SparseCore 0:
  40.0 100.3 all-gather.1
  289.2 82.5 reduce-scatter.6
  380.4 85.5 reduce-scatter.8
